TPU v7x, 32 devices: a whole 2x2x4 slice. The times are simulated.
32 devices in a mesh: occ: 4 (over y, x), vir: 8 (over z, core).
Axes of the slice: x: 2, y: 2, z: 4, core: 2. Of those that a mesh axis runs over, the one named last changes fastest.
Arguments:
- amplitudes: bfloat16 [64, 8, 64, 4096], P(None, 'vir', 'occ'), may hold values from -6 to 6
- integrals: bfloat16 [64, 32, 64, 4096], P(None, None, 'occ', 'vir'), may hold values from -0.01171875 to 0.01171875
- screen: int32 [8, 64, 64], P('vir', 'occ'), may hold values from 0 to 1, as said below
Outputs:
- cycle: bfloat16 [512, 2048], P(('occ', 'vir'))
Inputs may be any that keep to these rules, and one draw needn't show every extreme that they name: screen[a, k, t] is 1 where the amplitudes of first virtual a, occupied k and virtual tile t (virtuals t * 64 to (t + 1) * 64 - 1) survive screening, else 0.
All inputs are finite; a program needn't handle non-finite values.
Results may differ from a plain program's by a relative error of at most 0.001.
Values may be sent and summed in bfloat16 or wider, within the bound.
No kernel may reach another device: no remote copies, remote signals or barrier semaphores. Data moves between devices by JAX's collectives and lax.ppermute only.
A program may use at most 192 MiB of HBM per device.

v0:
```python
import jax
import jax.numpy as jnp
from jax import lax
from jax.sharding import PartitionSpec as P

TILE = 64


def on_device(amplitudes, integrals, screen):
    keep_mask = jnp.repeat(screen, TILE, axis=2).astype(jnp.bfloat16)
    screened = amplitudes * keep_mask[None]
    columns = integrals.shape[0] * integrals.shape[1]
    flat_weights = integrals.reshape(columns, -1)
    relaid = lax.all_to_all(screened, "vir", split_axis=3, concat_axis=1, tiled=True)
    left_rows = relaid.reshape(-1, flat_weights.shape[1])
    product = lax.dot_general(
        left_rows, flat_weights, (((1,), (1,)), ((), ())), preferred_element_type=jnp.float32
    )
    partial_value = product.reshape(relaid.shape[0], relaid.shape[1], columns)
    flat_rows = partial_value.reshape(-1, columns)
    owned_rows = lax.psum_scatter(flat_rows, ("occ", "vir"), scatter_dimension=0, tiled=True)
    return owned_rows.astype(jnp.bfloat16)


def solution(mesh):
    return jax.shard_map(
        on_device,
        mesh=mesh,
        in_specs=(P(None, "vir", "occ", None), P(None, None, "occ", "vir"), P("vir", "occ", None)),
        out_specs=P(("occ", "vir"), None),
        check_vma=False,
    )
```

profile of v0, /device:TPU:0, one launch (start us, length us, event | category | flops | bytes accessed | tf_op | source)
XLA Modules:
  0.0 468.2 jit_solution(5763869784065365802)
XLA Ops:
  6.5 0.7 convert_bitcast_fusion
  7.2 0.1 copy.11
  7.3 26.7 %copy.12 = bf16[64,1,16,4096]{0,2,1,3:T(8,128)(2,1)} copy(bf16[64,1,16,4096]{3,2,1,0:T(8,128)(2,1)} %param.3) | data formatting | bytes 16777216 | tf_op args[0]
  34.0 0.1 broadcast_in_dim.4
  34.2 14.8 %fusion = bf16[4096,1,16,64]{3,2,1,0:T(8,128)(2,1)} fusion(bf16[64,1,16,4096]{0,2,1,3:T(8,128)(2,1)} %copy.12, bf16[16,4096]{0,1:T(8,128)(2,1)S(1)} %bitcast.19), kind=kLoop, calls=%fused_computation.2 | loop fusion | flops 4194304 | bytes 16908288
  49.0 16.9 %reshape.26 = bf16[8,2,262144]{2,1,0:T(2,128)(2,1)} reshape(bf16[4096,1,16,64]{3,2,1,0:T(8,128)(2,1)} %fusion) | data formatting | bytes 16777216
  65.8 6.3 %all-to-all-start = ((bf16[8,2,262144]{2,1,0:T(2,128)(2,1)}), bf16[8,2,262144]{2,1,0:T(2,128)(2,1)}, u32[]{:S(2)}, u32[]{:S(2)}) async-start(bf16[8,2,262144]{2,1,0:T(2,128)(2,1)} %reshape.26), calls=%async_computation | async-start | bytes 16777216 | tf_op jit(solution)/shard_map/all_to_all | solution.py:14
  72.1 0.2 reduce-scatter.2.cloned.1.call-start
  72.4 31.0 %copy.15 = bf16[256,8,16,512]{3,1,2,0:T(8,128)(2,1)} copy(bf16[256,8,16,512]{3,2,1,0:T(8,128)(2,1)} %bitcast.16) | data formatting | bytes 67108864
  103.4 152.8 %all-to-all-done = bf16[8,2,262144]{2,1,0:T(2,128)(2,1)} async-done(((bf16[8,2,262144]{2,1,0:T(2,128)(2,1)}), bf16[8,2,262144]{2,1,0:T(2,128)(2,1)}, u32[]{:S(2)}, u32[]{:S(2)}) %all-to-all-start) | async-done | bytes 8388640 | tf_op jit(solution)/shard_map/all_to_all | solution.py:14
  256.1 16.5 %reshape.27 = bf16[4096,1,16,64]{3,2,1,0:T(8,128)(2,1)} reshape(bf16[8,2,262144]{2,1,0:T(2,128)(2,1)} %all-to-all-done) | data formatting | bytes 16777216
  272.6 20.7 %copy.14 = bf16[64,1,16,8,512]{4,3,2,0,1:T(8,128)(2,1)} copy(bf16[64,1,16,8,512]{0,2,4,3,1:T(8,128)(2,1)} %bitcast.15) | data formatting | bytes 16777216 | tf_op jit(solution)/shard_map/all_to_all | solution.py:14
  293.4 24.9 %fusion.1 = f32[512,2048]{1,0:T(8,128)} fusion(bf16[512,8192]{1,0:T(8,128)(2,1)} %bitcast.18, bf16[2048,8192]{1,0:T(8,128)(2,1)} %bitcast.17), kind=kOutput, calls=%fused_computation.3 | convolution fusion | flops 17179869184 | bytes 46137344 | tf_op jit(solution)/shard_map/dot_general | solution.py:16
  318.2 0.0 reduce-scatter.2.cloned.1.call-update
  318.3 141.5 %reduce-scatter.2.cloned.1.call-done = f32[16,2048]{1,0:T(8,128)} async-done(((f32[512,2048]{1,0:T(8,128)}), f32[16,2048]{1,0:T(8,128)}) %reduce-scatter.2.cloned.1.call-update) | async-done | bytes 131088 | tf_op jit(solution)/shard_map/reduce_scatter | solution.py:21
  459.8 1.5 convert_element_type.22
Async XLA Ops:
  65.8 190.3 %all-to-all-start = ((bf16[8,2,262144]{2,1,0:T(2,128)(2,1)}), bf16[8,2,262144]{2,1,0:T(2,128)(2,1)}, u32[]{:S(2)}, u32[]{:S(2)}) async-start(bf16[8,2,262144]{2,1,0:T(2,128)(2,1)} %reshape.26), calls=%async_computation | async-start | bytes 16777216 | tf_op jit(solution)/shard_map/all_to_all | solution.py:14
  72.1 387.6 %reduce-scatter.2.cloned.1.call-start = ((), (), s32[]{:S(2)}) async-start(), calls=%async_computation.2 | async-start | bytes 4325376 | tf_op jit(solution)/shard_map/reduce_scatter | solution.py:21
Sparse Core Ops, SparseCore 0:
  318.4 141.3 reduce-scatter.1
where the time goes:
time: 469 us; the launch traced here: 468 us
  waiting for transfers between devices  294 us (63%)
  local copies, waits for them, and re-layouts  112 us (24%)
  matrix products  24.9 us (5%)
  other arithmetic  17 us (4%)
  between operations  13.4 us (3%)
  starting transfers between devices  6.54 us (1%)
    all_to_all x1, waiting for transfers between devices, on_device(): lax.all_to_all(screened, 'vir', split_axis=3, concat_axis=1, tiled=True)  153 us
    reduce_scatter x1, waiting for transfers between devices, on_device(): lax.psum_scatter(flat_rows, ('occ', 'vir'), scatter_dimension=0, tiled=True)  142 us
    unnamed x4, local copies, waits for them, and re-layouts  91 us
    dot_general x1, matrix products, on_device(): lax.dot_general(left_rows, flat_weights, (((1,), (1,)), ((), ())), prefer...  24.9 us
    all_to_all x1, local copies, waits for them, and re-layouts, on_device(): lax.all_to_all(screened, 'vir', split_axis=3, concat_axis=1, tiled=True)  20.7 us
    unnamed x1, other arithmetic  14.8 us
  transfers between devices with their start and end apart: 2, of which 2 were waited for; matrix products, arithmetic and copies ran while one was open for 7% of the time, Pallas kernels for 0%

commit v1 on v0

v1 whole, which is shorter than its diff:
```python
import jax
import jax.numpy as jnp
from jax import lax
from jax.experimental import pallas as pl
from jax.experimental.pallas import tpu as pltpu
from jax.sharding import PartitionSpec as P

TILE = 64
MIB = 1 << 20


def screen_kernel(amp_ref, screen_ref, out_ref):
    depth, width = amp_ref.shape[-2:]
    dest = pl.program_id(0)
    tiles = screen_ref.shape[-1]
    tile_at = lax.broadcasted_iota(jnp.int32, (tiles, width), 0)
    column = lax.broadcasted_iota(jnp.int32, (tiles, width), 1) + dest * width
    spread = (column // TILE == tile_at).astype(jnp.float32).astype(jnp.bfloat16)
    mask = jnp.dot(
        screen_ref[0].astype(jnp.float32).astype(jnp.bfloat16), spread, preferred_element_type=jnp.float32
    ).astype(jnp.bfloat16)
    block = amp_ref[...].reshape(-1, depth, width) * mask[None]
    out_ref[0] = jnp.swapaxes(block, 0, 1)


def screened_part(amplitudes, screen, part, n_occ, n_vir):
    depth, total = amplitudes.shape[2:]
    width = total // n_vir
    view = amplitudes.reshape(n_occ, n_vir // 2, 2, 2, depth, total)
    rows = n_occ * n_vir // 2
    return pl.pallas_call(
        screen_kernel,
        grid=(n_vir, 2),
        in_specs=[
            pl.BlockSpec((n_occ, n_vir // 2, 1, 1, depth, width), lambda d, c: (0, 0, c, part, 0, d)),
            pl.BlockSpec(screen.shape, lambda d, c: (0, 0, 0)),
        ],
        out_specs=pl.BlockSpec((1, depth, rows, width), lambda d, c: (d, 0, c, 0)),
        out_shape=jax.ShapeDtypeStruct((n_vir, depth, 2 * rows, width), jnp.bfloat16),
        compiler_params=pltpu.CompilerParams(vmem_limit_bytes=32 * MIB),
        name="screen_amplitudes",
    )(view, screen)


def product_kernel(left_ref, weight_ref, out_ref):
    sources, depth, rows, width = left_ref.shape
    total = None
    for k in range(depth):
        left = left_ref[:, k].reshape(sources * rows, width)
        term = lax.dot_general(
            left, weight_ref[k], (((1,), (1,)), ((), ())), preferred_element_type=jnp.float32
        )
        total = term if total is None else total + term
    half = rows // 2
    total = total.reshape(sources, 2, half, total.shape[-1])
    out_ref[0] = total[:, 0]
    out_ref[1] = total[:, 1]


def product(left, weights, block):
    sources, depth, rows, width = left.shape
    columns = weights.shape[1]
    return pl.pallas_call(
        product_kernel,
        grid=(columns // block,),
        in_specs=[
            pl.BlockSpec(left.shape, lambda n: (0, 0, 0, 0)),
            pl.BlockSpec((depth, block, width), lambda n: (0, n, 0)),
        ],
        out_specs=pl.BlockSpec((2, sources, rows // 2, block), lambda n: (0, 0, 0, n)),
        out_shape=jax.ShapeDtypeStruct((2, sources, rows // 2, columns), jnp.float32),
        compiler_params=pltpu.CompilerParams(vmem_limit_bytes=48 * MIB),
        cost_estimate=pl.CostEstimate(
            flops=2 * sources * rows * depth * width * columns,
            bytes_accessed=2 * (left.size + weights.size) + 4 * sources * rows * columns,
            transcendentals=0,
        ),
        name="product",
    )(left, weights)


def pick(x, at, axis):
    return lax.dynamic_index_in_dim(x, at, axis, keepdims=False)


def exchange(x, axis_name, step, size):
    return lax.ppermute(x, axis_name, [(j, j ^ step) for j in range(size)])


def owned(partial_sums, n_occ, n_vir):
    cores, firsts, _, columns = partial_sums.shape
    vir, occ = lax.axis_index("vir"), lax.axis_index("occ")
    core, z = vir % 2, vir // 2
    held = pick(partial_sums, core, 0) + exchange(pick(partial_sums, 1 - core, 0), "vir", 1, n_vir)
    n_z = n_vir // 2
    held = held.reshape(firsts, n_occ, n_z, columns)
    total = pick(held, occ, 1)
    for s in range(1, n_occ):
        total = total + exchange(pick(held, occ ^ s, 1), "occ", s, n_occ)
    held = total
    total = pick(held, z, 1)
    for s in range(1, n_z):
        total = total + exchange(pick(held, z ^ s, 1), "vir", 2 * s, n_vir)
    return total.astype(jnp.bfloat16)


def on_block(amplitudes, integrals, screen, n_occ, n_vir):
    columns = integrals.shape[0] * integrals.shape[1]
    weights = integrals.reshape(columns, *integrals.shape[2:]).swapaxes(0, 1)
    done = []
    for part in range(2):
        mine = screened_part(amplitudes, screen, part, n_occ, n_vir)
        left = lax.all_to_all(mine, "vir", 0, 0, tiled=True)
        done.append(owned(product(left, weights, 256), n_occ, n_vir))
    return jnp.stack(done).reshape(-1, columns)


def on_any(amplitudes, integrals, screen):
    keep_mask = jnp.repeat(screen, TILE, axis=2).astype(jnp.bfloat16)
    screened = amplitudes * keep_mask[None]
    columns = integrals.shape[0] * integrals.shape[1]
    flat_weights = integrals.reshape(columns, -1)
    relaid = lax.all_to_all(screened, "vir", split_axis=3, concat_axis=1, tiled=True)
    left_rows = relaid.reshape(-1, flat_weights.shape[1])
    partial_value = lax.dot_general(
        left_rows, flat_weights, (((1,), (1,)), ((), ())), preferred_element_type=jnp.float32
    )
    owned_rows = lax.psum_scatter(partial_value, ("occ", "vir"), scatter_dimension=0, tiled=True)
    return owned_rows.astype(jnp.bfloat16)


def solution(mesh):
    n_occ, n_vir = mesh.shape["occ"], mesh.shape["vir"]

    def on_device(amplitudes, integrals, screen):
        fits = n_occ == 4 and n_vir == 8
        if fits and amplitudes.shape[0] == 2 * n_occ * n_vir and amplitudes.shape[1] == 1:
            return on_block(amplitudes, integrals, screen, n_occ, n_vir)
        return on_any(amplitudes, integrals, screen)

    return jax.shard_map(
        on_device,
        mesh=mesh,
        in_specs=(P(None, "vir", "occ", None), P(None, None, "occ", "vir"), P("vir", "occ", None)),
        out_specs=P(("occ", "vir"), None),
        check_vma=False,
    )
```

time: 469 us -> 266 us (0.57)
  waiting for transfers between devices: 294 us -> 152 us
  local copies, waits for them, and re-layouts: 112 us -> 38.2 us
  Pallas kernels: 0 us -> 42.4 us
  matrix products: 24.9 us -> 0 us
  starting transfers between devices: 6.54 us -> 28.4 us
  other arithmetic: 17 us -> 3.8 us
  between operations: 13.4 us -> 0.28 us
    reduce_scatter x1 -> x0, waiting for transfers between devices: 142 us -> none  [on_device(): lax.psum_scatter(flat_rows, ('occ', 'vir'), scatter_dimension=0, tiled=True)]
    unnamed x4 -> x15, local copies, waits for them, and re-layouts: 91 us -> 35.6 us
    pallas_call x0 -> x4, Pallas kernels: none -> 42.4 us  [the longest x2 34.2 us: product(): pl.pallas_call(product_kernel, grid=(columns // block,), in_specs=[pl.Blo...]
    dot_general x1 -> x0, matrix products: 24.9 us -> none  [on_device(): lax.dot_general(left_rows, flat_weights, (((1,), (1,)), ((), ())), prefer...]
    all_to_all x1 -> x0, local copies, waits for them, and re-layouts: 20.7 us -> none  [on_device(): lax.all_to_all(screened, 'vir', split_axis=3, concat_axis=1, tiled=True)]
    ppermute x0 -> x14, starting transfers between devices: none -> 17.4 us  [exchange(): return lax.ppermute(x, axis_name, [(j, j ^ step) for j in range(size)])]
    all_to_all x1 -> x2, waiting for transfers between devices: 153 us -> 136 us  [on_block(): left = lax.all_to_all(mine, 'vir', 0, 0, tiled=True)]
    ppermute x0 -> x14, waiting for transfers between devices: none -> 16.2 us  [exchange(): return lax.ppermute(x, axis_name, [(j, j ^ step) for j in range(size)])]
  transfers between devices with their start and end apart: 2 -> 16, of which waited for: 2 -> 7; matrix products, arithmetic and copies ran while one was open for 7% -> 11% of each run, Pallas kernels for 0% -> 14%
where the time goes in v1:
time: 266 us; the launch traced here: 265 us
  waiting for transfers between devices  152 us (57%)
  Pallas kernels  42.4 us (16%)
  local copies, waits for them, and re-layouts  38.2 us (14%)
  starting transfers between devices  28.4 us (11%)
  other arithmetic  3.8 us (1%)
    all_to_all x2, waiting for transfers between devices, on_block(): left = lax.all_to_all(mine, 'vir', 0, 0, tiled=True)  136 us
    unnamed x15, local copies, waits for them, and re-layouts  35.6 us
    pallas_call x2, Pallas kernels, product(): pl.pallas_call(product_kernel, grid=(columns // block,), in_specs=[pl.Blo...  34.2 us
    ppermute x14, starting transfers between devices, exchange(): return lax.ppermute(x, axis_name, [(j, j ^ step) for j in range(size)])  17.4 us
    ppermute x14, waiting for transfers between devices, exchange(): return lax.ppermute(x, axis_name, [(j, j ^ step) for j in range(size)])  16.2 us
    all_to_all x2, starting transfers between devices, on_block(): left = lax.all_to_all(mine, 'vir', 0, 0, tiled=True)  11 us
    pallas_call x2, Pallas kernels, screened_part(): pl.pallas_call(screen_kernel, grid=(n_vir, 2), in_specs=[pl.BlockSpec((n_...  8.16 us
  transfers between devices with their start and end apart: 16, of which 7 were waited for; matrix products, arithmetic and copies ran while one was open for 11% of the time, Pallas kernels for 14%

profile of v1, /device:TPU:0, one launch (start us, length us, event | category | flops | bytes accessed | tf_op | source)
XLA Modules:
  0.0 265.2 jit_solution(1444172297648636545)
XLA Ops:
  0.0 3.4 %copy-done = bf16[64,1,16,4096]{3,2,1,0:T(8,128)(2,1)S(1)} copy-done((bf16[64,1,16,4096]{3,2,1,0:T(8,128)(2,1)S(1)}, bf16[64,1,16,4096]{3,2,1,0:T(8,128)(2,1)}, u32[]{:S(2)}) %copy-start) | copy-done | bytes 8388632
  4.1 4.1 %screen_amplitudes.2 = bf16[8,16,32,512]{3,2,1,0:T(8,128)(2,1)S(1)} custom-call(bf16[4,4,2,2,16,4096]{5,4,3,2,1,0:T(8,128)(2,1)S(1)} %bitcast.76, s32[1,16,64]{2,1,0:T(8,128)S(1)} %copy-done.5), custom_call_target="tpu_custom_call" | custom-call | tf_op jit(solution)/shard_map/screen_amplitudes/pallas_call | solution.py:31
  8.2 2.0 copy-done.3
  10.2 6.5 %all-to-all-start = ((bf16[8,16,32,512]{3,2,1,0:T(8,128)(2,1)}), bf16[8,16,32,512]{3,2,1,0:T(8,128)(2,1)}, u32[]{:S(2)}, u32[]{:S(2)}) async-start(bf16[8,16,32,512]{3,2,1,0:T(8,128)(2,1)} %copy-done.3), calls=%async_computation | async-start | bytes 8388608 | tf_op jit(solution)/shard_map/all_to_all | solution.py:113
  16.7 3.4 %copy-done.1 = bf16[64,1,16,4096]{3,2,1,0:T(8,128)(2,1)S(1)} copy-done((bf16[64,1,16,4096]{3,2,1,0:T(8,128)(2,1)S(1)}, bf16[64,1,16,4096]{3,2,1,0:T(8,128)(2,1)}, u32[]{:S(2)}) %copy-start.1) | copy-done | bytes 8388632
  20.0 4.1 %screen_amplitudes.3 = bf16[8,16,32,512]{3,2,1,0:T(8,128)(2,1)S(1)} custom-call(bf16[4,4,2,2,16,4096]{5,4,3,2,1,0:T(8,128)(2,1)S(1)} %bitcast.77, s32[1,16,64]{2,1,0:T(8,128)S(1)} %copy-done.6), custom_call_target="tpu_custom_call" | custom-call | tf_op jit(solution)/shard_map/screen_amplitudes/pallas_call | solution.py:31
  24.1 2.1 copy-done.2
  26.2 84.6 %all-to-all-done.left_ref = bf16[8,16,32,512]{3,2,1,0:T(8,128)(2,1)} async-done(((bf16[8,16,32,512]{3,2,1,0:T(8,128)(2,1)}), bf16[8,16,32,512]{3,2,1,0:T(8,128)(2,1)}, u32[]{:S(2)}, u32[]{:S(2)}) %all-to-all-start) | async-done | bytes 4194336 | tf_op jit(solution)/shard_map/all_to_all | solution.py:113
  110.8 4.6 %all-to-all-start.1 = ((bf16[8,16,32,512]{3,2,1,0:T(8,128)(2,1)}), bf16[8,16,32,512]{3,2,1,0:T(8,128)(2,1)}, u32[]{:S(2)}, u32[]{:S(2)}) async-start(bf16[8,16,32,512]{3,2,1,0:T(8,128)(2,1)} %copy-done.2), calls=%async_computation.1 | async-start | bytes 8388608 | tf_op jit(solution)/shard_map/all_to_all | solution.py:113
  115.3 22.7 %copy.6 = bf16[64,32,16,512]{3,1,0,2:T(8,128)(2,1)} copy(bf16[64,32,16,512]{3,2,1,0:T(8,128)(2,1)} %param.4) | data formatting | bytes 67108864 | tf_op args[1]
  138.1 17.1 %product.2 = f32[2,8,16,2048]{3,2,1,0:T(8,128)S(1)} custom-call(bf16[8,16,32,512]{3,2,1,0:T(8,128)(2,1)} %all-to-all-done.left_ref, bf16[16,2048,512]{2,1,0:T(8,128)(2,1)} %bitcast.78), custom_call_target="tpu_custom_call" | custom-call | flops 8589934592 | bytes 39845888 | tf_op jit(solution)/shard_map/product/pallas_call | solution.py:63
  158.0 51.3 %all-to-all-done.1.left_ref = bf16[8,16,32,512]{3,2,1,0:T(8,128)(2,1)} async-done(((bf16[8,16,32,512]{3,2,1,0:T(8,128)(2,1)}), bf16[8,16,32,512]{3,2,1,0:T(8,128)(2,1)}, u32[]{:S(2)}, u32[]{:S(2)}) %all-to-all-start.1) | async-done | bytes 4194336 | tf_op jit(solution)/shard_map/all_to_all | solution.py:113
  209.3 17.1 %product.3 = f32[2,8,16,2048]{3,2,1,0:T(8,128)S(1)} custom-call(bf16[8,16,32,512]{3,2,1,0:T(8,128)(2,1)} %all-to-all-done.1.left_ref, bf16[16,2048,512]{2,1,0:T(8,128)(2,1)} %bitcast.79), custom_call_target="tpu_custom_call" | custom-call | flops 8589934592 | bytes 39845888 | tf_op jit(solution)/shard_map/product/pallas_call | solution.py:63
  226.7 1.7 bitcast_add_fusion.1
  229.0 1.6 collective-permute-start.1
  230.6 1.5 collective-permute-start.2
  234.6 2.5 collective-permute-start.10
  238.2 1.5 collective-permute-start.9
  239.7 10.4 %collective-permute-done.2 = f32[8,4,2048]{2,0,1:T(8,128)S(1)} collective-permute-done((f32[8,4,2048]{2,0,1:T(8,128)S(1)}, f32[8,4,2048]{2,0,1:T(8,128)S(1)}, u32[]{:S(2)}, u32[]{:S(2)}) %collective-permute-start.2) | collective-permute-done | bytes 262176 | tf_op jit(solution)/shard_map/ppermute | solution.py:87
  250.3 1.8 collective-permute-start.5
  252.1 2.6 collective-permute-start.6
  256.0 1.8 collective-permute-start.12
  257.8 2.6 collective-permute-start.13
  261.1 3.4 %collective-permute-done.12 = f32[8,2048]{1,0:T(8,128)S(1)} collective-permute-done((f32[8,2048]{1,0:T(8,128)S(1)}, f32[8,2048]{1,0:T(8,128)S(1)}, u32[]{:S(2)}, u32[]{:S(2)}) %collective-permute-start.12) | collective-permute-done | bytes 65568 | tf_op jit(solution)/shard_map/ppermute | solution.py:87
  (42 shorter events, 10.8 us)
Async XLA Ops:
  0.0 3.4 %copy-start = (bf16[64,1,16,4096]{3,2,1,0:T(8,128)(2,1)S(1)}, bf16[64,1,16,4096]{3,2,1,0:T(8,128)(2,1)}, u32[]{:S(2)}) copy-start(bf16[64,1,16,4096]{3,2,1,0:T(8,128)(2,1)} %param.3) | copy-start | bytes 25165828
  3.4 0.7 copy-start.5
  8.2 2.0 copy-start.3
  10.2 6.5 %copy-start.6 = (s32[1,16,64]{2,1,0:T(8,128)S(1)}, s32[1,16,64]{2,1,0:T(8,128)}, u32[]{:S(2)}) copy-start(s32[1,16,64]{2,1,0:T(8,128)} %screen_ref.3) | copy-start | bytes 12292
  10.2 100.6 %all-to-all-start = ((bf16[8,16,32,512]{3,2,1,0:T(8,128)(2,1)}), bf16[8,16,32,512]{3,2,1,0:T(8,128)(2,1)}, u32[]{:S(2)}, u32[]{:S(2)}) async-start(bf16[8,16,32,512]{3,2,1,0:T(8,128)(2,1)} %copy-done.3), calls=%async_computation | async-start | bytes 8388608 | tf_op jit(solution)/shard_map/all_to_all | solution.py:113
  16.6 3.4 %copy-start.1 = (bf16[64,1,16,4096]{3,2,1,0:T(8,128)(2,1)S(1)}, bf16[64,1,16,4096]{3,2,1,0:T(8,128)(2,1)}, u32[]{:S(2)}) copy-start(bf16[64,1,16,4096]{3,2,1,0:T(8,128)(2,1)} %param.3) | copy-start | bytes 25165828
  24.1 2.1 copy-start.2
  110.8 98.6 %all-to-all-start.1 = ((bf16[8,16,32,512]{3,2,1,0:T(8,128)(2,1)}), bf16[8,16,32,512]{3,2,1,0:T(8,128)(2,1)}, u32[]{:S(2)}, u32[]{:S(2)}) async-start(bf16[8,16,32,512]{3,2,1,0:T(8,128)(2,1)} %copy-done.2), calls=%async_computation.1 | async-start | bytes 8388608 | tf_op jit(solution)/shard_map/all_to_all | solution.py:113
  155.2 1.4 copy-start.4
  157.6 69.0 %collective-permute-start = (f32[8,16,2048]{2,1,0:T(8,128)}, f32[8,16,2048]{2,1,0:T(8,128)}, u32[]{:S(2)}, u32[]{:S(2)}) collective-permute-start(f32[8,16,2048]{2,1,0:T(8,128)} %dynamic-slice_bitcast_fusion.1), channel_id=1, source_target_pairs={{0,1},{1,0},{2,3},{3,2},{4,5},{5,4},{6,7},{7,6},{8,9},{9,8},{10,11... | collective-permute-start | bytes 3145736 | tf_op jit(solution)/shard_map/ppermute | solution.py:87
  226.5 6.1 %collective-permute-start.7 = (f32[8,16,2048]{2,1,0:T(8,128)S(1)}, f32[8,16,2048]{2,1,0:T(8,128)}, u32[]{:S(2)}, u32[]{:S(2)}) collective-permute-start(f32[8,16,2048]{2,1,0:T(8,128)S(1)} %dynamic-slice_bitcast_fusion), channel_id=1, source_target_pairs={{0,1},{1,0},{2,3},{3,2},{4,5},{5,4},{6,7},{7,6},{8,9},{9,8},{10,11... | collective-permute-start | bytes 3145736 | tf_op jit(solution)/shard_map/ppermute | solution.py:87
  229.0 9.2 %collective-permute-start.1 = (f32[8,4,2048]{2,0,1:T(8,128)S(1)}, f32[8,4,2048]{2,0,1:T(8,128)S(1)}, u32[]{:S(2)}, u32[]{:S(2)}) collective-permute-start(f32[8,4,2048]{2,0,1:T(8,128)S(1)} %get-tuple-element.5), channel_id=1, source_target_pairs={{0,8},{8,0},{16,24},{24,16},{1,9},{9,1},{17,25},{25,17},{2,10},{10... | collective-permute-start | bytes 786440 | tf_op jit(solution)/shard_map/ppermute | solution.py:87
  230.6 19.5 %collective-permute-start.2 = (f32[8,4,2048]{2,0,1:T(8,128)S(1)}, f32[8,4,2048]{2,0,1:T(8,128)S(1)}, u32[]{:S(2)}, u32[]{:S(2)}) collective-permute-start(f32[8,4,2048]{2,0,1:T(8,128)S(1)} %get-tuple-element.7), channel_id=1, source_target_pairs={{0,16},{8,24},{16,0},{24,8},{1,17},{9,25},{17,1},{25,9},{2,18},{10... | collective-permute-start | bytes 786440 | tf_op jit(solution)/shard_map/ppermute | solution.py:87
  232.1 18.0 %collective-permute-start.3 = (f32[8,4,2048]{2,0,1:T(8,128)S(1)}, f32[8,4,2048]{2,0,1:T(8,128)S(1)}, u32[]{:S(2)}, u32[]{:S(2)}) collective-permute-start(f32[8,4,2048]{2,0,1:T(8,128)S(1)} %get-tuple-element.6), channel_id=1, source_target_pairs={{0,24},{8,16},{16,8},{24,0},{1,25},{9,17},{17,9},{25,1},{2,26},{10... | collective-permute-start | bytes 786440 | tf_op jit(solution)/shard_map/ppermute | solution.py:87
  234.6 17.4 %collective-permute-start.10 = (f32[8,4,2048]{2,0,1:T(8,128)S(1)}, f32[8,4,2048]{2,0,1:T(8,128)S(1)}, u32[]{:S(2)}, u32[]{:S(2)}) collective-permute-start(f32[8,4,2048]{2,0,1:T(8,128)S(1)} %get-tuple-element.9), channel_id=1, source_target_pairs={{0,24},{8,16},{16,8},{24,0},{1,25},{9,17},{17,9},{25,1},{2,26},{10... | collective-permute-start | bytes 786440 | tf_op jit(solution)/shard_map/ppermute | solution.py:87
  237.1 17.5 %collective-permute-start.8 = (f32[8,4,2048]{2,0,1:T(8,128)S(1)}, f32[8,4,2048]{2,0,1:T(8,128)S(1)}, u32[]{:S(2)}, u32[]{:S(2)}) collective-permute-start(f32[8,4,2048]{2,0,1:T(8,128)S(1)} %get-tuple-element.8), channel_id=1, source_target_pairs={{0,8},{8,0},{16,24},{24,16},{1,9},{9,1},{17,25},{25,17},{2,10},{10... | collective-permute-start | bytes 786440 | tf_op jit(solution)/shard_map/ppermute | solution.py:87
  238.2 17.6 %collective-permute-start.9 = (f32[8,4,2048]{2,0,1:T(8,128)S(1)}, f32[8,4,2048]{2,0,1:T(8,128)S(1)}, u32[]{:S(2)}, u32[]{:S(2)}) collective-permute-start(f32[8,4,2048]{2,0,1:T(8,128)S(1)} %get-tuple-element.10), channel_id=1, source_target_pairs={{0,16},{8,24},{16,0},{24,8},{1,17},{9,25},{17,1},{25,9},{2,18},{10... | collective-permute-start | bytes 786440 | tf_op jit(solution)/shard_map/ppermute | solution.py:87
  250.2 7.6 %collective-permute-start.4 = (f32[8,2048]{1,0:T(8,128)S(1)}, f32[8,2048]{1,0:T(8,128)S(1)}, u32[]{:S(2)}, u32[]{:S(2)}) collective-permute-start(f32[8,2048]{1,0:T(8,128)S(1)} %get-tuple-element.11), channel_id=1, source_target_pairs={{0,2},{1,3},{2,0},{3,1},{4,6},{5,7},{6,4},{7,5},{8,10},{9,11},{10,... | collective-permute-start | bytes 196616 | tf_op jit(solution)/shard_map/ppermute | solution.py:87
  250.3 10.1 %collective-permute-start.5 = (f32[8,2048]{1,0:T(8,128)S(1)}, f32[8,2048]{1,0:T(8,128)S(1)}, u32[]{:S(2)}, u32[]{:S(2)}) collective-permute-start(f32[8,2048]{1,0:T(8,128)S(1)} %get-tuple-element.13), channel_id=1, source_target_pairs={{0,4},{1,5},{2,6},{3,7},{4,0},{5,1},{6,2},{7,3},{8,12},{9,13},{10,... | collective-permute-start | bytes 196616 | tf_op jit(solution)/shard_map/ppermute | solution.py:87
  252.1 8.3 %collective-permute-start.6 = (f32[8,2048]{1,0:T(8,128)S(1)}, f32[8,2048]{1,0:T(8,128)S(1)}, u32[]{:S(2)}, u32[]{:S(2)}) collective-permute-start(f32[8,2048]{1,0:T(8,128)S(1)} %get-tuple-element.12), channel_id=1, source_target_pairs={{0,6},{1,7},{2,4},{3,5},{4,2},{5,3},{6,0},{7,1},{8,14},{9,15},{10,... | collective-permute-start | bytes 196616 | tf_op jit(solution)/shard_map/ppermute | solution.py:87
  255.9 5.2 %collective-permute-start.11 = (f32[8,2048]{1,0:T(8,128)S(1)}, f32[8,2048]{1,0:T(8,128)S(1)}, u32[]{:S(2)}, u32[]{:S(2)}) collective-permute-start(f32[8,2048]{1,0:T(8,128)S(1)} %get-tuple-element.14), channel_id=1, source_target_pairs={{0,2},{1,3},{2,0},{3,1},{4,6},{5,7},{6,4},{7,5},{8,10},{9,11},{10,... | collective-permute-start | bytes 196616 | tf_op jit(solution)/shard_map/ppermute | solution.py:87
  256.0 8.5 %collective-permute-start.12 = (f32[8,2048]{1,0:T(8,128)S(1)}, f32[8,2048]{1,0:T(8,128)S(1)}, u32[]{:S(2)}, u32[]{:S(2)}) collective-permute-start(f32[8,2048]{1,0:T(8,128)S(1)} %get-tuple-element.16), channel_id=1, source_target_pairs={{0,4},{1,5},{2,6},{3,7},{4,0},{5,1},{6,2},{7,3},{8,12},{9,13},{10,... | collective-permute-start | bytes 196616 | tf_op jit(solution)/shard_map/ppermute | solution.py:87
  257.8 6.7 %collective-permute-start.13 = (f32[8,2048]{1,0:T(8,128)S(1)}, f32[8,2048]{1,0:T(8,128)S(1)}, u32[]{:S(2)}, u32[]{:S(2)}) collective-permute-start(f32[8,2048]{1,0:T(8,128)S(1)} %get-tuple-element.15), channel_id=1, source_target_pairs={{0,6},{1,7},{2,4},{3,5},{4,2},{5,3},{6,0},{7,1},{8,14},{9,15},{10,... | collective-permute-start | bytes 196616 | tf_op jit(solution)/shard_map/ppermute | solution.py:87

commit v2 on v0

v2 whole, which is shorter than its diff:
```python
import functools

import jax
import jax.numpy as jnp
from jax import lax
from jax.experimental import pallas as pl
from jax.experimental.pallas import tpu as pltpu
from jax.sharding import PartitionSpec as P

TILE = 64
VMEM = 60 << 20


def screen_block(amp, screen_ref, dest):
    depth, width = amp.shape[-2:]
    tiles = screen_ref.shape[-1]
    tile_at = lax.broadcasted_iota(jnp.int32, (tiles, width), 0)
    column = lax.broadcasted_iota(jnp.int32, (tiles, width), 1) + dest * width
    spread = (column // TILE == tile_at).astype(jnp.float32).astype(jnp.bfloat16)
    rows = screen_ref[0].astype(jnp.float32).astype(jnp.bfloat16)
    mask = jnp.dot(rows, spread, preferred_element_type=jnp.float32).astype(jnp.bfloat16)
    return jnp.swapaxes(amp.reshape(-1, depth, width) * mask[None], 0, 1)


def screen_kernel(*refs, dests):
    screen_ref, out_ref = refs[dests], refs[-1]
    for dest in range(dests):
        out_ref[dest] = screen_block(refs[dest][...], screen_ref, dest)


def screened_part(amplitudes, screen, part, n_occ, n_vir):
    depth, total = amplitudes.shape[2:]
    width, rows = total // n_vir, n_occ * n_vir // 2
    view = amplitudes.reshape(n_occ, n_vir // 2, 2, 2, depth, total)
    some = depth // 2

    def source(dest):
        return pl.BlockSpec((n_occ, n_vir // 2, 1, 1, some, width), lambda c, k: (0, 0, c, part, k, dest))

    return pl.pallas_call(
        functools.partial(screen_kernel, dests=n_vir),
        grid=(2, 2),
        in_specs=[source(dest) for dest in range(n_vir)]
        + [pl.BlockSpec((1, some, screen.shape[2]), lambda c, k: (0, k, 0))],
        out_specs=pl.BlockSpec((n_vir, some, rows, width), lambda c, k: (0, k, c, 0)),
        out_shape=jax.ShapeDtypeStruct((n_vir, depth, 2 * rows, width), jnp.bfloat16),
        compiler_params=pltpu.CompilerParams(vmem_limit_bytes=VMEM),
        cost_estimate=pl.CostEstimate(flops=0, bytes_accessed=0, transcendentals=0),
        name="screen",
    )(*[view] * n_vir, screen)


def product_kernel(me_ref, left_ref, weight_ref, *refs):
    mine_ref, give_ref = refs[-2:]
    units, depth, rows, width = left_ref.shape
    piece = mine_ref.shape[1]
    total = None
    for k in range(depth):
        term = lax.dot_general(
            left_ref[:, k].reshape(units * rows, width),
            weight_ref[k],
            (((1,), (1,)), ((), ())),
            preferred_element_type=jnp.float32,
        )
        total = term if total is None else total + term
    odd = me_ref[0] % 2 == 1
    for unit in range(units):
        zero, one = (total[unit * rows + core * piece : unit * rows + (core + 1) * piece] for core in range(2))
        mine_ref[unit] = jnp.where(odd, one, zero)
        give_ref[unit] = jnp.where(odd, zero, one)


def product(left, weights, first, count, block, after=(), limit=VMEM, cost=0):
    units, depth, rows, width = left.shape
    out = jax.ShapeDtypeStruct((units, rows // 2, count), jnp.float32)
    out_spec = pl.BlockSpec((units, rows // 2, block), lambda n, at: (0, 0, n))
    return pl.pallas_call(
        product_kernel,
        grid_spec=pltpu.PrefetchScalarGridSpec(
            num_scalar_prefetch=1,
            grid=(count // block,),
            in_specs=[
                pl.BlockSpec(left.shape, lambda n, at: (0, 0, 0, 0)),
                pl.BlockSpec((depth, block, width), lambda n, at: (0, first // block + n, 0)),
                *[pl.BlockSpec(memory_space=pl.ANY) for _ in after],
            ],
            out_specs=[out_spec, out_spec],
        ),
        out_shape=[out, out],
        compiler_params=pltpu.CompilerParams(vmem_limit_bytes=limit),
        cost_estimate=pl.CostEstimate(flops=cost, bytes_accessed=0, transcendentals=0),
        name="product",
    )(lax.axis_index("vir").astype(jnp.int32).reshape(1), left, weights, *after)


def pick(x, at, axis):
    return lax.dynamic_index_in_dim(x, at, axis, keepdims=False)


def exchange(x, axis_name, step, size):
    return lax.ppermute(x, axis_name, [(j, j ^ step) for j in range(size)])


def in_plane(mine, give, n_occ, n_vir):
    occ, n_z = lax.axis_index("occ"), n_vir // 2
    held = mine + exchange(give, "vir", 1, n_vir)
    held = held.reshape(held.shape[0], n_occ, n_z, held.shape[-1])
    total = pick(held, occ, 1)
    for s in range(1, n_occ):
        total = total + exchange(pick(held, occ ^ s, 1), "occ", s, n_occ)
    return total


def along_z(total, n_vir):
    z, n_z = lax.axis_index("vir") // 2, n_vir // 2
    out = pick(total, z, 1)
    for s in range(1, n_z):
        out = out + exchange(pick(total, z ^ s, 1), "vir", 2 * s, n_vir)
    return out


def on_block(amplitudes, integrals, screen, n_occ, n_vir):
    columns = integrals.shape[0] * integrals.shape[1]
    weights = integrals.reshape(columns, *integrals.shape[2:]).swapaxes(0, 1)
    cuts = 1
    count = columns // cuts
    left = [
        lax.all_to_all(screened_part(amplitudes, screen, part, n_occ, n_vir), "vir", 0, 0, tiled=True)
        for part in range(2)
    ]
    first = in_plane(*product(left[0], weights, 0, columns, 512), n_occ, n_vir)
    last, after = [], (first,)
    for cut in range(cuts):
        mine, give = product(left[1], weights, cut * count, count, 512, after, limit=VMEM, cost=0)
        after = (first, give)
        last.append(in_plane(mine, give, n_occ, n_vir))
    last = [along_z(x, n_vir) for x in last]
    done = jnp.stack([along_z(first, n_vir), jnp.concatenate(last, axis=1)])
    return done.astype(jnp.bfloat16).reshape(-1, columns)


def on_any(amplitudes, integrals, screen):
    keep_mask = jnp.repeat(screen, TILE, axis=2).astype(jnp.bfloat16)
    screened = amplitudes * keep_mask[None]
    columns = integrals.shape[0] * integrals.shape[1]
    flat_weights = integrals.reshape(columns, -1)
    relaid = lax.all_to_all(screened, "vir", split_axis=3, concat_axis=1, tiled=True)
    left_rows = relaid.reshape(-1, flat_weights.shape[1])
    partial_value = lax.dot_general(
        left_rows, flat_weights, (((1,), (1,)), ((), ())), preferred_element_type=jnp.float32
    )
    owned_rows = lax.psum_scatter(partial_value, ("occ", "vir"), scatter_dimension=0, tiled=True)
    return owned_rows.astype(jnp.bfloat16)


def solution(mesh):
    n_occ, n_vir = mesh.shape["occ"], mesh.shape["vir"]

    def on_device(amplitudes, integrals, screen):
        fits = n_occ == 4 and n_vir == 8
        if fits and amplitudes.shape[0] == 2 * n_occ * n_vir and amplitudes.shape[1] == 1:
            return on_block(amplitudes, integrals, screen, n_occ, n_vir)
        return on_any(amplitudes, integrals, screen)

    return jax.shard_map(
        on_device,
        mesh=mesh,
        in_specs=(P(None, "vir", "occ", None), P(None, None, "occ", "vir"), P("vir", "occ", None)),
        out_specs=P(("occ", "vir"), None),
        check_vma=False,
    )
```

time: 469 us -> 251 us (0.54)
  waiting for transfers between devices: 294 us -> 151 us
  local copies, waits for them, and re-layouts: 112 us -> 24.1 us
  Pallas kernels: 0 us -> 44.5 us
  matrix products: 24.9 us -> 0 us
  starting transfers between devices: 6.54 us -> 26 us
  between operations: 13.4 us -> 0.13 us
  other arithmetic: 17 us -> 4.25 us
    reduce_scatter x1 -> x0, waiting for transfers between devices: 142 us -> none  [on_device(): lax.psum_scatter(flat_rows, ('occ', 'vir'), scatter_dimension=0, tiled=True)]
    unnamed x4 -> x6, local copies, waits for them, and re-layouts: 91 us -> 22.8 us
    pallas_call x0 -> x4, Pallas kernels: none -> 44.5 us  [the longest x2 33.1 us: product(): pl.pallas_call(product_kernel, grid_spec=pltpu.PrefetchScalarGridSpec(num...]
    all_to_all x1 -> x2, waiting for transfers between devices: 153 us -> 122 us  [on_block(): lax.all_to_all(screened_part(amplitudes, screen, part, n_occ, n_vir), 'vi...]
    ppermute x0 -> x14, waiting for transfers between devices: none -> 29.2 us  [exchange(): return lax.ppermute(x, axis_name, [(j, j ^ step) for j in range(size)])]
    dot_general x1 -> x0, matrix products: 24.9 us -> none  [on_device(): lax.dot_general(left_rows, flat_weights, (((1,), (1,)), ((), ())), prefer...]
    all_to_all x1 -> x0, local copies, waits for them, and re-layouts: 20.7 us -> none  [on_device(): lax.all_to_all(screened, 'vir', split_axis=3, concat_axis=1, tiled=True)]
    ppermute x0 -> x14, starting transfers between devices: none -> 15.1 us  [exchange(): return lax.ppermute(x, axis_name, [(j, j ^ step) for j in range(size)])]
  transfers between devices with their start and end apart: 2 -> 16, of which waited for: 2 -> 10; matrix products, arithmetic and copies ran while one was open for 7% -> 10% of each run, Pallas kernels for 0% -> 9%
where the time goes in v2:
time: 251 us; the launch traced here: 250 us
  waiting for transfers between devices  151 us (60%)
  Pallas kernels  44.5 us (18%)
  starting transfers between devices  26 us (10%)
  local copies, waits for them, and re-layouts  24.1 us (10%)
  other arithmetic  4.25 us (2%)
    all_to_all x2, waiting for transfers between devices, on_block(): lax.all_to_all(screened_part(amplitudes, screen, part, n_occ, n_vir), 'vi...  122 us
    pallas_call x2, Pallas kernels, product(): pl.pallas_call(product_kernel, grid_spec=pltpu.PrefetchScalarGridSpec(num...  33.1 us
    ppermute x14, waiting for transfers between devices, exchange(): return lax.ppermute(x, axis_name, [(j, j ^ step) for j in range(size)])  29.2 us
    unnamed x6, local copies, waits for them, and re-layouts  22.8 us
    ppermute x14, starting transfers between devices, exchange(): return lax.ppermute(x, axis_name, [(j, j ^ step) for j in range(size)])  15.1 us
    pallas_call x2, Pallas kernels, screened_part(): pl.pallas_call(functools.partial(screen_kernel, dests=n_vir), grid=(2, 2)...  11.4 us
    all_to_all x2, starting transfers between devices, on_block(): lax.all_to_all(screened_part(amplitudes, screen, part, n_occ, n_vir), 'vi...  10.9 us
  transfers between devices with their start and end apart: 16, of which 10 were waited for; matrix products, arithmetic and copies ran while one was open for 10% of the time, Pallas kernels for 9%

profile of v2, /device:TPU:0, one launch (start us, length us, event | category | flops | bytes accessed | tf_op | source)
XLA Modules:
  0.0 250.4 jit_solution(1709627351282795456)
XLA Ops:
  0.0 5.7 %screen.2 = bf16[8,16,32,512]{3,2,1,0:T(8,128)(2,1)} custom-call(bf16[4,4,2,2,16,4096]{5,4,3,2,1,0:T(8,128)(2,1)} %bitcast.79, bf16[4,4,2,2,16,4096]{5,4,3,2,1,0:T(8,128)(2,1)} %bitcast.80, bf16[4,4,2,2,16,4096]{5,4,3,2,1,0:T(8,128)(2,1)} %bitcast.81, bf16[4,4,2,2,16,4096]{5,4,3,2,1,0:T(8,128)(2,1)} %bitcast.82, bf16[4,4,2,2,16,4096]{5,4,3,2,1,0:T(8,128)(2,1)} %bitcast.83, ...), custom_call_target="tpu_custom_call" | custom-call | tf_op jit(solution)/shard_map/screen/pallas_call | solution.py:40
  5.7 6.3 %all-to-all-start = ((bf16[8,16,32,512]{3,2,1,0:T(8,128)(2,1)}), bf16[8,16,32,512]{3,2,1,0:T(8,128)(2,1)}, u32[]{:S(2)}, u32[]{:S(2)}) async-start(bf16[8,16,32,512]{3,2,1,0:T(8,128)(2,1)} %screen.2), calls=%async_computation | async-start | bytes 8388608 | tf_op jit(solution)/shard_map/all_to_all | solution.py:128
  12.0 5.7 %screen.3 = bf16[8,16,32,512]{3,2,1,0:T(8,128)(2,1)} custom-call(bf16[4,4,2,2,16,4096]{5,4,3,2,1,0:T(8,128)(2,1)} %bitcast.87, bf16[4,4,2,2,16,4096]{5,4,3,2,1,0:T(8,128)(2,1)} %bitcast.88, bf16[4,4,2,2,16,4096]{5,4,3,2,1,0:T(8,128)(2,1)} %bitcast.89, bf16[4,4,2,2,16,4096]{5,4,3,2,1,0:T(8,128)(2,1)} %bitcast.90, bf16[4,4,2,2,16,4096]{5,4,3,2,1,0:T(8,128)(2,1)} %bitcast.91, ...), custom_call_target="tpu_custom_call" | custom-call | tf_op jit(solution)/shard_map/screen/pallas_call | solution.py:40
  17.7 88.4 %all-to-all-done.left_ref = bf16[8,16,32,512]{3,2,1,0:T(8,128)(2,1)} async-done(((bf16[8,16,32,512]{3,2,1,0:T(8,128)(2,1)}), bf16[8,16,32,512]{3,2,1,0:T(8,128)(2,1)}, u32[]{:S(2)}, u32[]{:S(2)}) %all-to-all-start) | async-done | bytes 4194336 | tf_op jit(solution)/shard_map/all_to_all | solution.py:128
  106.1 4.5 %all-to-all-start.1 = ((bf16[8,16,32,512]{3,2,1,0:T(8,128)(2,1)}), bf16[8,16,32,512]{3,2,1,0:T(8,128)(2,1)}, u32[]{:S(2)}, u32[]{:S(2)}) async-start(bf16[8,16,32,512]{3,2,1,0:T(8,128)(2,1)} %screen.3), calls=%async_computation.1 | async-start | bytes 8388608 | tf_op jit(solution)/shard_map/all_to_all | solution.py:128
  110.7 22.7 %copy.9 = bf16[64,32,16,512]{3,1,0,2:T(8,128)(2,1)} copy(bf16[64,32,16,512]{3,2,1,0:T(8,128)(2,1)} %param.4) | data formatting | bytes 67108864 | tf_op args[1]
  133.4 16.6 %product.2 = (f32[8,16,2048]{2,1,0:T(8,128)}, f32[8,16,2048]{2,1,0:T(8,128)}) custom-call(s32[1]{0:T(128)} %bitcast.me_ref, bf16[8,16,32,512]{3,2,1,0:T(8,128)(2,1)} %all-to-all-done.left_ref, bf16[16,2048,512]{2,1,0:T(8,128)(2,1)} %bitcast.95), custom_call_target="tpu_custom_call" | custom-call | tf_op jit(solution)/shard_map/product/pallas_call | solution.py:77
  150.3 2.5 %collective-permute-done = f32[8,16,2048]{2,1,0:T(8,128)S(1)} collective-permute-done((f32[8,16,2048]{2,1,0:T(8,128)}, f32[8,16,2048]{2,1,0:T(8,128)S(1)}, u32[]{:S(2)}, u32[]{:S(2)}) %collective-permute-start) | collective-permute-done | bytes 1048608 | tf_op jit(solution)/shard_map/ppermute | solution.py:101
  152.8 1.3 add.77
  154.6 1.6 collective-permute-start.1
  156.1 1.5 collective-permute-start.2
  158.1 5.6 %collective-permute-done.1 = f32[8,4,2048]{2,1,0:T(4,128)S(1)} collective-permute-done((f32[8,4,2048]{2,1,0:T(4,128)S(1)}, f32[8,4,2048]{2,1,0:T(4,128)S(1)}, u32[]{:S(2)}, u32[]{:S(2)}) %collective-permute-start.1) | collective-permute-done | bytes 262176 | tf_op jit(solution)/shard_map/ppermute | solution.py:101
  163.8 6.3 %collective-permute-done.2 = f32[8,4,2048]{2,1,0:T(4,128)S(1)} collective-permute-done((f32[8,4,2048]{2,1,0:T(4,128)S(1)}, f32[8,4,2048]{2,1,0:T(4,128)S(1)}, u32[]{:S(2)}, u32[]{:S(2)}) %collective-permute-start.2) | collective-permute-done | bytes 262176 | tf_op jit(solution)/shard_map/ppermute | solution.py:101
  170.9 33.8 %all-to-all-done.1.left_ref = bf16[8,16,32,512]{3,2,1,0:T(8,128)(2,1)} async-done(((bf16[8,16,32,512]{3,2,1,0:T(8,128)(2,1)}), bf16[8,16,32,512]{3,2,1,0:T(8,128)(2,1)}, u32[]{:S(2)}, u32[]{:S(2)}) %all-to-all-start.1) | async-done | bytes 4194336 | tf_op jit(solution)/shard_map/all_to_all | solution.py:128
  204.7 16.6 %product.3 = (f32[8,16,2048]{2,1,0:T(8,128)}, f32[8,16,2048]{2,1,0:T(8,128)}) custom-call(s32[1]{0:T(128)} %bitcast.me_ref, bf16[8,16,32,512]{3,2,1,0:T(8,128)(2,1)} %all-to-all-done.1.left_ref, bf16[16,2048,512]{2,1,0:T(8,128)(2,1)} %bitcast.96, f32[8,4,2048]{2,1,0:T(4,128)} %fusion.1.refs_0_), custom_call_target="tpu_custom_call" | custom-call | tf_op jit(solution)/shard_map/product/pallas_call | solution.py:77
  221.2 2.9 %collective-permute-done.7 = f32[8,16,2048]{2,1,0:T(8,128)S(1)} collective-permute-done((f32[8,16,2048]{2,1,0:T(8,128)}, f32[8,16,2048]{2,1,0:T(8,128)S(1)}, u32[]{:S(2)}, u32[]{:S(2)}) %collective-permute-start.7) | collective-permute-done | bytes 1048608 | tf_op jit(solution)/shard_map/ppermute | solution.py:101
  224.1 1.3 add.92
  226.1 2.5 %collective-permute-start.10 = (f32[8,4,2048]{2,0,1:T(8,128)S(1)}, f32[8,4,2048]{2,0,1:T(8,128)S(1)}, u32[]{:S(2)}, u32[]{:S(2)}) collective-permute-start(f32[8,4,2048]{2,0,1:T(8,128)S(1)} %get-tuple-element.14), channel_id=1, source_target_pairs={{0,24},{8,16},{16,8},{24,0},{1,25},{9,17},{17,9},{25,1},{2,26},{10... | collective-permute-start | bytes 786440 | tf_op jit(solution)/shard_map/ppermute | solution.py:101
  230.1 1.8 collective-permute-start.5
  232.0 4.3 %collective-permute-done.10 = f32[8,4,2048]{2,0,1:T(8,128)S(1)} collective-permute-done((f32[8,4,2048]{2,0,1:T(8,128)S(1)}, f32[8,4,2048]{2,0,1:T(8,128)S(1)}, u32[]{:S(2)}, u32[]{:S(2)}) %collective-permute-start.10) | collective-permute-done | bytes 262176 | tf_op jit(solution)/shard_map/ppermute | solution.py:101
  237.5 3.6 %collective-permute-done.8 = f32[8,4,2048]{2,0,1:T(8,128)S(1)} collective-permute-done((f32[8,4,2048]{2,0,1:T(8,128)S(1)}, f32[8,4,2048]{2,0,1:T(8,128)S(1)}, u32[]{:S(2)}, u32[]{:S(2)}) %collective-permute-start.8) | collective-permute-done | bytes 262176 | tf_op jit(solution)/shard_map/ppermute | solution.py:101
  241.3 1.8 collective-permute-start.12
  243.1 2.6 %collective-permute-start.13 = (f32[8,2048]{1,0:T(8,128)S(1)}, f32[8,2048]{1,0:T(8,128)S(1)}, u32[]{:S(2)}, u32[]{:S(2)}) collective-permute-start(f32[8,2048]{1,0:T(8,128)S(1)} %get-tuple-element.24), channel_id=1, source_target_pairs={{0,6},{1,7},{2,4},{3,5},{4,2},{5,3},{6,0},{7,1},{8,14},{9,15},{10,... | collective-permute-start | bytes 196616 | tf_op jit(solution)/shard_map/ppermute | solution.py:101
  246.3 3.4 %collective-permute-done.12 = f32[8,2048]{1,0:T(8,128)S(1)} collective-permute-done((f32[8,2048]{1,0:T(8,128)S(1)}, f32[8,2048]{1,0:T(8,128)S(1)}, u32[]{:S(2)}, u32[]{:S(2)}) %collective-permute-start.12) | collective-permute-done | bytes 65568 | tf_op jit(solution)/shard_map/ppermute | solution.py:101
  (31 shorter events, 6.8 us)
Async XLA Ops:
  5.7 100.4 %all-to-all-start = ((bf16[8,16,32,512]{3,2,1,0:T(8,128)(2,1)}), bf16[8,16,32,512]{3,2,1,0:T(8,128)(2,1)}, u32[]{:S(2)}, u32[]{:S(2)}) async-start(bf16[8,16,32,512]{3,2,1,0:T(8,128)(2,1)} %screen.2), calls=%async_computation | async-start | bytes 8388608 | tf_op jit(solution)/shard_map/all_to_all | solution.py:128
  106.1 98.6 %all-to-all-start.1 = ((bf16[8,16,32,512]{3,2,1,0:T(8,128)(2,1)}), bf16[8,16,32,512]{3,2,1,0:T(8,128)(2,1)}, u32[]{:S(2)}, u32[]{:S(2)}) async-start(bf16[8,16,32,512]{3,2,1,0:T(8,128)(2,1)} %screen.3), calls=%async_computation.1 | async-start | bytes 8388608 | tf_op jit(solution)/shard_map/all_to_all | solution.py:128
  150.0 2.9 %collective-permute-start = (f32[8,16,2048]{2,1,0:T(8,128)}, f32[8,16,2048]{2,1,0:T(8,128)S(1)}, u32[]{:S(2)}, u32[]{:S(2)}) collective-permute-start(f32[8,16,2048]{2,1,0:T(8,128)} %get-tuple-element.10), channel_id=1, source_target_pairs={{0,1},{1,0},{2,3},{3,2},{4,5},{5,4},{6,7},{7,6},{8,9},{9,8},{10,11... | collective-permute-start | bytes 3145736 | tf_op jit(solution)/shard_map/ppermute | solution.py:101
  154.6 9.2 %collective-permute-start.1 = (f32[8,4,2048]{2,1,0:T(4,128)S(1)}, f32[8,4,2048]{2,1,0:T(4,128)S(1)}, u32[]{:S(2)}, u32[]{:S(2)}) collective-permute-start(f32[8,4,2048]{2,1,0:T(4,128)S(1)} %get-tuple-element.16), channel_id=1, source_target_pairs={{0,8},{8,0},{16,24},{24,16},{1,9},{9,1},{17,25},{25,17},{2,10},{10... | collective-permute-start | bytes 786440 | tf_op jit(solution)/shard_map/ppermute | solution.py:101
  156.1 13.9 %collective-permute-start.2 = (f32[8,4,2048]{2,1,0:T(4,128)S(1)}, f32[8,4,2048]{2,1,0:T(4,128)S(1)}, u32[]{:S(2)}, u32[]{:S(2)}) collective-permute-start(f32[8,4,2048]{2,1,0:T(4,128)S(1)} %get-tuple-element.17), channel_id=1, source_target_pairs={{0,16},{8,24},{16,0},{24,8},{1,17},{9,25},{17,1},{25,9},{2,18},{10... | collective-permute-start | bytes 786440 | tf_op jit(solution)/shard_map/ppermute | solution.py:101
  157.7 12.4 %collective-permute-start.3 = (f32[8,4,2048]{2,1,0:T(4,128)S(1)}, f32[8,4,2048]{2,1,0:T(4,128)S(1)}, u32[]{:S(2)}, u32[]{:S(2)}) collective-permute-start(f32[8,4,2048]{2,1,0:T(4,128)S(1)} %get-tuple-element.18), channel_id=1, source_target_pairs={{0,24},{8,16},{16,8},{24,0},{1,25},{9,17},{17,9},{25,1},{2,26},{10... | collective-permute-start | bytes 786440 | tf_op jit(solution)/shard_map/ppermute | solution.py:101
  221.2 8.5 %copy-start = (f32[8,4,2048]{2,1,0:T(4,128)S(1)}, f32[8,4,2048]{2,1,0:T(4,128)}, u32[]{:S(2)}) copy-start(f32[8,4,2048]{2,1,0:T(4,128)} %fusion.1.refs_0_) | copy-start | bytes 786436
  221.2 2.9 %collective-permute-start.7 = (f32[8,16,2048]{2,1,0:T(8,128)}, f32[8,16,2048]{2,1,0:T(8,128)S(1)}, u32[]{:S(2)}, u32[]{:S(2)}) collective-permute-start(f32[8,16,2048]{2,1,0:T(8,128)} %get-tuple-element.12), channel_id=1, source_target_pairs={{0,1},{1,0},{2,3},{3,2},{4,5},{5,4},{6,7},{7,6},{8,9},{9,8},{10,11... | collective-permute-start | bytes 3145736 | tf_op jit(solution)/shard_map/ppermute | solution.py:101
  226.1 10.2 %collective-permute-start.10 = (f32[8,4,2048]{2,0,1:T(8,128)S(1)}, f32[8,4,2048]{2,0,1:T(8,128)S(1)}, u32[]{:S(2)}, u32[]{:S(2)}) collective-permute-start(f32[8,4,2048]{2,0,1:T(8,128)S(1)} %get-tuple-element.14), channel_id=1, source_target_pairs={{0,24},{8,16},{16,8},{24,0},{1,25},{9,17},{17,9},{25,1},{2,26},{10... | collective-permute-start | bytes 786440 | tf_op jit(solution)/shard_map/ppermute | solution.py:101
  228.7 12.5 %collective-permute-start.8 = (f32[8,4,2048]{2,0,1:T(8,128)S(1)}, f32[8,4,2048]{2,0,1:T(8,128)S(1)}, u32[]{:S(2)}, u32[]{:S(2)}) collective-permute-start(f32[8,4,2048]{2,0,1:T(8,128)S(1)} %get-tuple-element.13), channel_id=1, source_target_pairs={{0,8},{8,0},{16,24},{24,16},{1,9},{9,1},{17,25},{25,17},{2,10},{10... | collective-permute-start | bytes 786440 | tf_op jit(solution)/shard_map/ppermute | solution.py:101
  229.2 12.0 %collective-permute-start.9 = (f32[8,4,2048]{2,0,1:T(8,128)S(1)}, f32[8,4,2048]{2,0,1:T(8,128)S(1)}, u32[]{:S(2)}, u32[]{:S(2)}) collective-permute-start(f32[8,4,2048]{2,0,1:T(8,128)S(1)} %get-tuple-element.15), channel_id=1, source_target_pairs={{0,16},{8,24},{16,0},{24,8},{1,17},{9,25},{17,1},{25,9},{2,18},{10... | collective-permute-start | bytes 786440 | tf_op jit(solution)/shard_map/ppermute | solution.py:101
  230.0 13.1 %collective-permute-start.4 = (f32[8,2048]{1,0:T(8,128)S(1)}, f32[8,2048]{1,0:T(8,128)S(1)}, u32[]{:S(2)}, u32[]{:S(2)}) collective-permute-start(f32[8,2048]{1,0:T(8,128)S(1)} %bitcast.101), channel_id=1, source_target_pairs={{0,2},{1,3},{2,0},{3,1},{4,6},{5,7},{6,4},{7,5},{8,10},{9,11},{10,... | collective-permute-start | bytes 196616 | tf_op jit(solution)/shard_map/ppermute | solution.py:101
  230.1 15.6 %collective-permute-start.5 = (f32[8,2048]{1,0:T(8,128)S(1)}, f32[8,2048]{1,0:T(8,128)S(1)}, u32[]{:S(2)}, u32[]{:S(2)}) collective-permute-start(f32[8,2048]{1,0:T(8,128)S(1)} %bitcast.99), channel_id=1, source_target_pairs={{0,4},{1,5},{2,6},{3,7},{4,0},{5,1},{6,2},{7,3},{8,12},{9,13},{10,... | collective-permute-start | bytes 196616 | tf_op jit(solution)/shard_map/ppermute | solution.py:101
  236.3 9.4 %collective-permute-start.6 = (f32[8,2048]{1,0:T(8,128)S(1)}, f32[8,2048]{1,0:T(8,128)S(1)}, u32[]{:S(2)}, u32[]{:S(2)}) collective-permute-start(f32[8,2048]{1,0:T(8,128)S(1)} %bitcast.100), channel_id=1, source_target_pairs={{0,6},{1,7},{2,4},{3,5},{4,2},{5,3},{6,0},{7,1},{8,14},{9,15},{10,... | collective-permute-start | bytes 196616 | tf_op jit(solution)/shard_map/ppermute | solution.py:101
  241.3 5.0 %collective-permute-start.11 = (f32[8,2048]{1,0:T(8,128)S(1)}, f32[8,2048]{1,0:T(8,128)S(1)}, u32[]{:S(2)}, u32[]{:S(2)}) collective-permute-start(f32[8,2048]{1,0:T(8,128)S(1)} %get-tuple-element.23), channel_id=1, source_target_pairs={{0,2},{1,3},{2,0},{3,1},{4,6},{5,7},{6,4},{7,5},{8,10},{9,11},{10,... | collective-permute-start | bytes 196616 | tf_op jit(solution)/shard_map/ppermute | solution.py:101
  241.3 8.4 %collective-permute-start.12 = (f32[8,2048]{1,0:T(8,128)S(1)}, f32[8,2048]{1,0:T(8,128)S(1)}, u32[]{:S(2)}, u32[]{:S(2)}) collective-permute-start(f32[8,2048]{1,0:T(8,128)S(1)} %get-tuple-element.25), channel_id=1, source_target_pairs={{0,4},{1,5},{2,6},{3,7},{4,0},{5,1},{6,2},{7,3},{8,12},{9,13},{10,... | collective-permute-start | bytes 196616 | tf_op jit(solution)/shard_map/ppermute | solution.py:101
  243.1 6.6 %collective-permute-start.13 = (f32[8,2048]{1,0:T(8,128)S(1)}, f32[8,2048]{1,0:T(8,128)S(1)}, u32[]{:S(2)}, u32[]{:S(2)}) collective-permute-start(f32[8,2048]{1,0:T(8,128)S(1)} %get-tuple-element.24), channel_id=1, source_target_pairs={{0,6},{1,7},{2,4},{3,5},{4,2},{5,3},{6,0},{7,1},{8,14},{9,15},{10,... | collective-permute-start | bytes 196616 | tf_op jit(solution)/shard_map/ppermute | solution.py:101

commit v3 on v2

v3 whole, which is shorter than its diff:
```python
import functools

import jax
import jax.numpy as jnp
from jax import lax
from jax.experimental import pallas as pl
from jax.experimental.pallas import tpu as pltpu
from jax.sharding import PartitionSpec as P

TILE = 64
VMEM = 60 << 20


def screen_block(amp, screen_ref, dest):
    depth, width = amp.shape[-2:]
    tiles = screen_ref.shape[-1]
    tile_at = lax.broadcasted_iota(jnp.int32, (tiles, width), 0)
    column = lax.broadcasted_iota(jnp.int32, (tiles, width), 1) + dest * width
    spread = (column // TILE == tile_at).astype(jnp.float32).astype(jnp.bfloat16)
    rows = screen_ref[0].astype(jnp.float32).astype(jnp.bfloat16)
    mask = jnp.dot(rows, spread, preferred_element_type=jnp.float32).astype(jnp.bfloat16)
    return jnp.swapaxes(amp.reshape(-1, depth, width) * mask[None], 0, 1)


def give_kernel(me_ref, amp_ref, screen_ref, *refs, steps):
    out_ref = refs[-1]
    step = steps[0]
    for at, other in enumerate(steps):
        step = jnp.where(pl.program_id(0) == at, other, step)
    out_ref[0] = screen_block(amp_ref[...], screen_ref, me_ref[0] ^ (2 * step + 1))


def keep_kernel(me_ref, *refs, steps, parts):
    screen_ref, given_refs = refs[len(steps)], refs[len(steps) + 1 : 2 * len(steps) + 1]
    out_refs = refs[len(refs) - len(steps) :]
    for at, step in enumerate(steps):
        out_refs[at][0] = screen_block(refs[at][...], screen_ref, me_ref[0] ^ (2 * step))
        out_refs[at][1] = given_refs[at][0]


def position():
    return lax.axis_index("vir").astype(jnp.int32).reshape(1)


def amplitude_view(amplitudes, n_occ, n_vir):
    return amplitudes.reshape(n_occ, n_vir // 2, 2, 2, *amplitudes.shape[2:])


def given(amplitudes, screen, units, n_occ, n_vir, after=()):
    depth, total = amplitudes.shape[2:]
    width, rows = total // n_vir, n_occ * n_vir // 2
    parts, steps = [u[0] for u in units], [u[1] for u in units]

    def choose(values, at):
        out = values[0]
        for n, value in enumerate(values):
            out = jnp.where(at == n, value, out)
        return out

    return pl.pallas_call(
        functools.partial(give_kernel, steps=steps),
        grid_spec=pltpu.PrefetchScalarGridSpec(
            num_scalar_prefetch=1,
            grid=(len(units), 2),
            in_specs=[
                pl.BlockSpec(
                    (n_occ, n_vir // 2, 1, 1, depth, width),
                    lambda u, c, at: (0, 0, c, choose(parts, u), 0, at[0] ^ (2 * choose(steps, u) + 1)),
                ),
                pl.BlockSpec(screen.shape, lambda u, c, at: (0, 0, 0)),
            ]
            + [pl.BlockSpec(memory_space=pl.ANY) for _ in after],
            out_specs=pl.BlockSpec((1, depth, rows, width), lambda u, c, at: (u, 0, c, 0)),
        ),
        out_shape=jax.ShapeDtypeStruct((len(units), depth, 2 * rows, width), jnp.bfloat16),
        compiler_params=pltpu.CompilerParams(vmem_limit_bytes=VMEM),
        cost_estimate=pl.CostEstimate(flops=0, bytes_accessed=0, transcendentals=0),
        name="give",
    )(position(), amplitude_view(amplitudes, n_occ, n_vir), screen, *after)


def kept(amplitudes, screen, got, first, parts, steps, base, n_occ, n_vir, after=()):
    depth, total = amplitudes.shape[2:]
    width, rows = total // n_vir, n_occ * n_vir // 2
    view = amplitude_view(amplitudes, n_occ, n_vir)

    def source(step):
        return pl.BlockSpec(
            (n_occ, n_vir // 2, 1, 1, depth, width), lambda p, c, at: (0, 0, c, first + p, 0, at[0] ^ (2 * step))
        )

    def sibling(n):
        return pl.BlockSpec((1, depth, rows, width), lambda p, c, at: (base + n * parts + p, 0, c, 0))

    return pl.pallas_call(
        functools.partial(keep_kernel, steps=steps, parts=parts),
        grid_spec=pltpu.PrefetchScalarGridSpec(
            num_scalar_prefetch=1,
            grid=(parts, 2),
            in_specs=[source(step) for step in steps]
            + [pl.BlockSpec(screen.shape, lambda p, c, at: (0, 0, 0))]
            + [sibling(n) for n in range(len(steps))]
            + [pl.BlockSpec(memory_space=pl.ANY) for _ in after],
            out_specs=[pl.BlockSpec((2, depth, rows, width), lambda p, c, at: (p, 0, c, 0)) for _ in steps],
        ),
        out_shape=[jax.ShapeDtypeStruct((2 * parts, depth, 2 * rows, width), jnp.bfloat16) for _ in steps],
        compiler_params=pltpu.CompilerParams(vmem_limit_bytes=VMEM),
        cost_estimate=pl.CostEstimate(flops=0, bytes_accessed=0, transcendentals=0),
        name="keep",
    )(position(), *[view] * len(steps), screen, *[got] * len(steps), *after)


def screen_kernel(*refs, dests):
    screen_ref, out_ref = refs[-2:]
    width = out_ref.shape[-1]
    per = screen_ref.shape[-1] // dests
    tile_at = lax.broadcasted_iota(jnp.int32, (per, width), 0)
    column = lax.broadcasted_iota(jnp.int32, (per, width), 1)
    spread = (column // TILE == tile_at).astype(jnp.float32).astype(jnp.bfloat16)
    rows = screen_ref[0].astype(jnp.float32).astype(jnp.bfloat16)
    for dest in range(dests):
        mask = jnp.dot(rows[:, dest * per : (dest + 1) * per], spread, preferred_element_type=jnp.float32)
        mask = mask.astype(jnp.bfloat16)[None]
        for core in range(2):
            block = refs[dest][:, :, core, 0]
            block = block.reshape(-1, *block.shape[2:])
            count = block.shape[0]
            out_ref[dest, :, core * count : (core + 1) * count] = jnp.swapaxes(block * mask, 0, 1)


def screened(amplitudes, screen, n_occ, n_vir):
    depth, total = amplitudes.shape[2:]
    width, n_z = total // n_vir, n_vir // 2
    some, rows = depth // 2, n_occ * n_vir

    def source(dest):
        return pl.BlockSpec((n_occ, n_z, 2, 1, some, width), lambda k: (0, 0, 0, 0, k, dest))

    return pl.pallas_call(
        functools.partial(screen_kernel, dests=n_vir),
        grid=(2,),
        in_specs=[source(dest) for dest in range(n_vir)]
        + [pl.BlockSpec((1, some, screen.shape[2]), lambda k: (0, k, 0))],
        out_specs=pl.BlockSpec((n_vir, some, rows, width), lambda k: (0, k, 0, 0)),
        out_shape=jax.ShapeDtypeStruct((n_vir, depth, rows, width), jnp.bfloat16),
        compiler_params=pltpu.CompilerParams(vmem_limit_bytes=VMEM),
        cost_estimate=pl.CostEstimate(flops=0, bytes_accessed=0, transcendentals=0),
        name="screen",
    )(*[amplitude_view(amplitudes, n_occ, n_vir)] * n_vir, screen)


def gate_kernel(*refs):
    del refs


def held_back(arrays, after):
    return pl.pallas_call(
        gate_kernel,
        in_specs=[pl.BlockSpec(memory_space=pl.ANY)] * (len(arrays) + len(after)),
        out_specs=[pl.BlockSpec(memory_space=pl.ANY)] * len(arrays),
        out_shape=[jax.ShapeDtypeStruct(x.shape, x.dtype) for x in arrays],
        input_output_aliases={n: n for n in range(len(arrays))},
        cost_estimate=pl.CostEstimate(flops=0, bytes_accessed=0, transcendentals=0),
        name="gate",
    )(*arrays, *after)


def product_kernel(me_ref, *refs, count, plain):
    left_refs, weight_ref, mine_ref, give_ref = refs[:count], refs[count], refs[-2], refs[-1]
    piece = mine_ref.shape[1]
    total = None
    for k in range(weight_ref.shape[0]):
        left = [ref[unit, k] for ref in left_refs for unit in range(ref.shape[0])]
        term = lax.dot_general(
            jnp.concatenate(left, axis=0),
            weight_ref[k],
            (((1,), (1,)), ((), ())),
            preferred_element_type=jnp.float32,
        )
        total = term if total is None else total + term
    odd = me_ref[0] % 2 == 1
    for unit in range(mine_ref.shape[0]):
        zero, one = (total[(2 * unit + core) * piece : (2 * unit + core + 1) * piece] for core in range(2))
        mine_ref[unit] = jnp.where(odd, one, zero)
        give_ref[unit if unit < plain else unit ^ 1] = jnp.where(odd, zero, one)


def product(lefts, weights, block, plain, turn=0, after=()):
    columns = weights.shape[1]
    shape = (sum(x.shape[0] for x in lefts), lefts[0].shape[2] // 2, columns)
    out_spec = pl.BlockSpec((*shape[:-1], block), lambda n, at: (0, 0, n))
    return pl.pallas_call(
        functools.partial(product_kernel, count=len(lefts), plain=plain),
        grid_spec=pltpu.PrefetchScalarGridSpec(
            num_scalar_prefetch=1,
            grid=(columns // block,),
            in_specs=[pl.BlockSpec(x.shape, lambda n, at: (0, 0, 0, 0)) for x in lefts]
            + [pl.BlockSpec((weights.shape[0], block, weights.shape[2]), lambda n, at: (0, n, 0))]
            + [pl.BlockSpec(memory_space=pl.ANY) for _ in after],
            out_specs=[out_spec, out_spec],
        ),
        out_shape=[jax.ShapeDtypeStruct(shape, jnp.float32)] * 2,
        compiler_params=pltpu.CompilerParams(vmem_limit_bytes=VMEM),
        cost_estimate=pl.CostEstimate(flops=0, bytes_accessed=0, transcendentals=0),
        name="product",
    )(position() + 2 * turn, *lefts, weights, *after)


def pick(x, at, axis):
    return lax.dynamic_index_in_dim(x, at, axis, keepdims=False)


def exchange(x, axis_name, step, size):
    return lax.ppermute(x, axis_name, [(j, j ^ step) for j in range(size)])


def over_cores(mine, give, n_occ, n_vir):
    held = mine + exchange(give, "vir", 1, n_vir)
    return held.reshape(held.shape[0], n_occ, n_vir // 2, held.shape[-1])


def over_plane(held, n_occ):
    occ = lax.axis_index("occ")
    total = pick(held, occ, 1)
    for s in range(1, n_occ):
        total = total + exchange(pick(held, occ ^ s, 1), "occ", s, n_occ)
    return total


def in_turn(held, index, axis_name, unit, size):
    step, count = 1, held.shape[1]
    while step < count:
        bit = (index // step) % 2
        parts = held.reshape(held.shape[0], -1, 2, *held.shape[2:])
        held = pick(parts, bit, 2) + exchange(pick(parts, 1 - bit, 2), axis_name, unit * step, size)
        step *= 2
    return held[:, 0]


def combine_kernel(me_ref, *refs, firsts):
    out_ref = refs[-1]
    n_z = len(refs) // 2
    plain = total = None
    for s in range(n_z):
        early = refs[s][...]
        value = jnp.concatenate([early[firsts:], refs[n_z + s][...]], axis=0)
        term = jnp.concatenate([value[m ^ 2 * s :][:1] for m in range(firsts)], axis=0) if s else value
        plain = plain + early[:firsts] if s else early[:firsts]
        total = total + term if s else term
    bit = 1
    while bit < firsts:
        other = jnp.concatenate([total[m ^ bit :][:1] for m in range(firsts)], axis=0)
        total = jnp.where((me_ref[0] & bit) != 0, other, total)
        bit *= 2
    out_ref[...] = jnp.concatenate([plain, total], axis=0).astype(out_ref.dtype)


def combined(early, late):
    columns = early[0].shape[1]
    firsts = (early[0].shape[0] + late[0].shape[0]) // 2
    block = columns // 2
    return pl.pallas_call(
        functools.partial(combine_kernel, firsts=firsts),
        grid_spec=pltpu.PrefetchScalarGridSpec(
            num_scalar_prefetch=1,
            grid=(columns // block,),
            in_specs=[pl.BlockSpec((x.shape[0], block), lambda n, at: (0, n)) for x in (*early, *late)],
            out_specs=pl.BlockSpec((2 * firsts, block), lambda n, at: (0, n)),
        ),
        out_shape=jax.ShapeDtypeStruct((2 * firsts, columns), jnp.bfloat16),
        name="combine",
    )(position(), *early, *late)


def along_z(sums, n_vir):
    z = lax.axis_index("vir") // 2
    return [pick(sums, z, 1)] + [exchange(pick(sums, z ^ s, 1), "vir", 2 * s, n_vir) for s in range(1, n_vir // 2)]


def on_block(amplitudes, integrals, screen, n_occ, n_vir):
    columns = integrals.shape[0] * integrals.shape[1]
    weights = integrals.reshape(columns, *integrals.shape[2:]).swapaxes(0, 1)
    n_z = n_vir // 2
    occ = lax.axis_index("occ")
    steps = list(range(n_z))
    soon, later = steps[:2], steps[2:]
    first = lax.all_to_all(screened(amplitudes, screen, n_occ, n_vir), "vir", 0, 0, tiled=True)

    give = given(amplitudes, screen, [(1, s) for s in steps], n_occ, n_vir, after=(weights,))
    got = exchange(give, "vir", 1, n_vir)
    last = []
    if soon:
        last += kept(amplitudes, screen, got, 1, 1, soon, 0, n_occ, n_vir)
    last += held_back(kept(amplitudes, screen, got, 1, 1, later, len(soon), n_occ, n_vir), (first,))
    last = [x if s == 0 else exchange(x, "vir", 2 * s, n_vir) for s, x in zip(steps, last)]

    def early(turn, _):
        held = over_cores(*product([first, *last[: len(soon)]], weights, 512, n_vir, turn), n_occ, n_vir)
        return in_turn(held, occ, "occ", 1, n_occ)

    once = 1 + lax.axis_index("vir") // n_vir
    units = n_vir + 2 * len(soon)
    early_sums = lax.fori_loop(0, once, early, jnp.zeros((units, n_z, columns), jnp.float32))
    mine, give = product(last[len(soon) :], weights, 512, 0, after=(early_sums,))
    late_sums = over_plane(over_cores(mine, give, n_occ, n_vir), n_occ)
    return combined(along_z(early_sums, n_vir), along_z(late_sums, n_vir))


def on_any(amplitudes, integrals, screen):
    keep_mask = jnp.repeat(screen, TILE, axis=2).astype(jnp.bfloat16)
    screened = amplitudes * keep_mask[None]
    columns = integrals.shape[0] * integrals.shape[1]
    flat_weights = integrals.reshape(columns, -1)
    relaid = lax.all_to_all(screened, "vir", split_axis=3, concat_axis=1, tiled=True)
    left_rows = relaid.reshape(-1, flat_weights.shape[1])
    partial_value = lax.dot_general(
        left_rows, flat_weights, (((1,), (1,)), ((), ())), preferred_element_type=jnp.float32
    )
    owned_rows = lax.psum_scatter(partial_value, ("occ", "vir"), scatter_dimension=0, tiled=True)
    return owned_rows.astype(jnp.bfloat16)


def solution(mesh):
    n_occ, n_vir = mesh.shape["occ"], mesh.shape["vir"]

    def on_device(amplitudes, integrals, screen):
        fits = n_occ == 4 and n_vir == 8
        if fits and amplitudes.shape[0] == 2 * n_occ * n_vir and amplitudes.shape[1] == 1:
            return on_block(amplitudes, integrals, screen, n_occ, n_vir)
        return on_any(amplitudes, integrals, screen)

    return jax.shard_map(
        on_device,
        mesh=mesh,
        in_specs=(P(None, "vir", "occ", None), P(None, None, "occ", "vir"), P("vir", "occ", None)),
        out_specs=P(("occ", "vir"), None),
        check_vma=False,
    )
```

time: 251 us -> 242 us (0.964)
  waiting for transfers between devices: 151 us -> 106 us
  starting transfers between devices: 26 us -> 47.2 us
  Pallas kernels: 44.5 us -> 55 us
  local copies, waits for them, and re-layouts: 24.1 us -> 28.5 us
    all_to_all x2 -> x1, waiting for transfers between devices: 122 us -> 51.6 us  [on_block(): lax.all_to_all(screened(amplitudes, screen, n_occ, n_vir), 'vir', 0, 0, t...]
    ppermute x14 -> x17, starting transfers between devices: 15.1 us -> 40.8 us  [exchange(): return lax.ppermute(x, axis_name, [(j, j ^ step) for j in range(size)])]
    ppermute x14 -> x17, waiting for transfers between devices: 29.2 us -> 54.7 us  [exchange(): return lax.ppermute(x, axis_name, [(j, j ^ step) for j in range(size)])]
    pallas_call x4 -> x8, Pallas kernels: 44.5 us -> 55 us  [the longest x2 36.9 us: product(): pl.pallas_call(functools.partial(product_kernel, count=len(lefts), plain=...]
    all_to_all x2 -> x1, starting transfers between devices: 10.9 us -> 6.34 us  [on_block(): lax.all_to_all(screened(amplitudes, screen, n_occ, n_vir), 'vir', 0, 0, t...]
    unnamed x6 -> x21, local copies, waits for them, and re-layouts: 22.8 us -> 25.5 us
  transfers between devices with their start and end apart: 16 -> 18, of which waited for: 10 -> 9; matrix products, arithmetic and copies ran while one was open for 10% -> 12% of each run, Pallas kernels for 9% -> 13%
where the time goes in v3:
time: 242 us; the launch traced here: 241 us
  waiting for transfers between devices  106 us (44%)
  Pallas kernels  55 us (23%)
  starting transfers between devices  47.2 us (20%)
  local copies, waits for them, and re-layouts  28.5 us (12%)
  other arithmetic  3.94 us (2%)
    ppermute x17, waiting for transfers between devices, exchange(): return lax.ppermute(x, axis_name, [(j, j ^ step) for j in range(size)])  54.7 us
    all_to_all x1, waiting for transfers between devices, on_block(): lax.all_to_all(screened(amplitudes, screen, n_occ, n_vir), 'vir', 0, 0, t...  51.6 us
    ppermute x17, starting transfers between devices, exchange(): return lax.ppermute(x, axis_name, [(j, j ^ step) for j in range(size)])  40.8 us
    pallas_call x2, Pallas kernels, product(): pl.pallas_call(functools.partial(product_kernel, count=len(lefts), plain=...  36.9 us
    unnamed x21, local copies, waits for them, and re-layouts  25.5 us
    pallas_call x1, Pallas kernels, given(): pl.pallas_call(functools.partial(give_kernel, steps=steps), grid_spec=plt...  6.39 us
    all_to_all x1, starting transfers between devices, on_block(): lax.all_to_all(screened(amplitudes, screen, n_occ, n_vir), 'vir', 0, 0, t...  6.34 us
    pallas_call x2, Pallas kernels, kept(): pl.pallas_call(functools.partial(keep_kernel, steps=steps, parts=parts),...  5.61 us
  transfers between devices with their start and end apart: 18, of which 9 were waited for; matrix products, arithmetic and copies ran while one was open for 12% of the time, Pallas kernels for 13%

profile of v3, /device:TPU:0, one launch (start us, length us, event | category | flops | bytes accessed | tf_op | source)
XLA Modules:
  0.0 241.1 jit_solution(16737804738654173822)
XLA Ops:
  0.0 4.3 %screen.1 = bf16[8,16,32,512]{3,2,1,0:T(8,128)(2,1)} custom-call(bf16[4,4,2,2,16,4096]{5,4,3,2,1,0:T(8,128)(2,1)} %bitcast.58, bf16[4,4,2,2,16,4096]{5,4,3,2,1,0:T(8,128)(2,1)} %bitcast.59, bf16[4,4,2,2,16,4096]{5,4,3,2,1,0:T(8,128)(2,1)} %bitcast.60, bf16[4,4,2,2,16,4096]{5,4,3,2,1,0:T(8,128)(2,1)} %bitcast.61, bf16[4,4,2,2,16,4096]{5,4,3,2,1,0:T(8,128)(2,1)} %bitcast.62, ...), custom_call_target="tpu_custom_call" | custom-call | tf_op jit(solution)/shard_map/screen/pallas_call | solution.py:139
  4.3 6.3 %all-to-all-start = ((bf16[8,16,32,512]{3,2,1,0:T(8,128)(2,1)}), bf16[8,16,32,512]{3,2,1,0:T(8,128)(2,1)}, u32[]{:S(2)}, u32[]{:S(2)}) async-start(bf16[8,16,32,512]{3,2,1,0:T(8,128)(2,1)} %screen.1), calls=%async_computation | async-start | bytes 8388608 | tf_op jit(solution)/shard_map/all_to_all | solution.py:287
  10.6 22.7 %copy.8 = bf16[64,32,16,512]{3,1,0,2:T(8,128)(2,1)} copy(bf16[64,32,16,512]{3,2,1,0:T(8,128)(2,1)} %param.6) | data formatting | bytes 67108864 | tf_op args[1]
  33.3 6.4 %give.1 = bf16[4,16,32,512]{3,2,1,0:T(8,128)(2,1)} custom-call(s32[1]{0:T(128)} %bitcast.4.me_ref, bf16[4,4,2,2,16,4096]{5,4,3,2,1,0:T(8,128)(2,1)} %bitcast.66, s32[1,16,64]{2,1,0:T(8,128)} %refs_2_.3, bf16[16,2048,512]{2,1,0:T(8,128)(2,1)} %bitcast.56), custom_call_target="tpu_custom_call" | custom-call | tf_op jit(solution)/shard_map/give/pallas_call | solution.py:60
  40.2 4.0 %collective-permute-done.3.refs_3_.refs_4_ = bf16[4,16,32,512]{3,2,1,0:T(8,128)(2,1)S(1)} collective-permute-done((bf16[4,16,32,512]{3,2,1,0:T(8,128)(2,1)}, bf16[4,16,32,512]{3,2,1,0:T(8,128)(2,1)S(1)}, u32[]{:S(2)}, u32[]{:S(2)}) %collective-permute-start.3) | collective-permute-done | bytes 2097184 | tf_op jit(solution)/shard_map/ppermute | solution.py:214
  45.6 2.7 %keep.2 = (bf16[2,16,32,512]{3,2,1,0:T(8,128)(2,1)S(1)}, bf16[2,16,32,512]{3,2,1,0:T(8,128)(2,1)}) custom-call(s32[1]{0:T(128)} %bitcast.4.me_ref, bf16[4,4,2,2,16,4096]{5,4,3,2,1,0:T(8,128)(2,1)} %bitcast.67, bf16[4,4,2,2,16,4096]{5,4,3,2,1,0:T(8,128)(2,1)} %bitcast.68, s32[1,16,64]{2,1,0:T(8,128)} %refs_2_.3, bf16[4,16,32,512]{3,2,1,0:T(8,128)(2,1)} %copy-done, ...), custom_call_target="tpu_custom_call" | custom-call | tf_op jit(solution)/shard_map/keep/pallas_call | solution.py:95
  48.3 1.9 collective-permute-start.4
  50.2 2.9 %keep.3 = (bf16[2,16,32,512]{3,2,1,0:T(8,128)(2,1)}, bf16[2,16,32,512]{3,2,1,0:T(8,128)(2,1)}) custom-call(s32[1]{0:T(128)} %bitcast.4.me_ref, bf16[4,4,2,2,16,4096]{5,4,3,2,1,0:T(8,128)(2,1)} %bitcast.69, bf16[4,4,2,2,16,4096]{5,4,3,2,1,0:T(8,128)(2,1)} %bitcast.70, s32[1,16,64]{2,1,0:T(8,128)} %refs_2_.3, bf16[4,16,32,512]{3,2,1,0:T(8,128)(2,1)} %copy-done, ...), custom_call_target="tpu_custom_call" | custom-call | tf_op jit(solution)/shard_map/keep/pallas_call | solution.py:95
  53.1 51.6 %all-to-all-done.refs_2_ = bf16[8,16,32,512]{3,2,1,0:T(8,128)(2,1)} async-done(((bf16[8,16,32,512]{3,2,1,0:T(8,128)(2,1)}), bf16[8,16,32,512]{3,2,1,0:T(8,128)(2,1)}, u32[]{:S(2)}, u32[]{:S(2)}) %all-to-all-start) | async-done | bytes 4194336 | tf_op jit(solution)/shard_map/all_to_all | solution.py:287
  106.9 57.4 %while.14 = (s32[]{:T(128)}, f32[12,4,2048]{2,1,0:T(4,128)}, s32[]{:T(128)}, bf16[8,16,32,512]{3,2,1,0:T(8,128)(2,1)}, bf16[2,16,32,512]{3,2,1,0:T(8,128)(2,1)S(...) while((s32[]{:T(128)}, f32[12,4,2048]{2,1,0:T(4,128)}, ...), condition=%wide.region_1.2_spmd, body=%wide.region_0.1_spmd.sunk | while | flops 688134 | bytes 36307312 | solution.py:303
  106.9 20.3 %product.7 = (f32[12,16,2048]{2,1,0:T(8,128)}, f32[12,16,2048]{2,1,0:T(8,128)}) custom-call(s32[1]{0:T(128)} %bitcast.54.me_ref, bf16[8,16,32,512]{3,2,1,0:T(8,128)(2,1)} %get-tuple-element.576.refs_0_, bf16[2,16,32,512]{3,2,1,0:T(8,128)(2,1)S(1)} %get-tuple-element.577.refs_1_, bf16[2,16,32,512]{3,2,1,0:T(8,128)(2,1)} %get-tuple-element.578.refs_2_, ...), custom_call_target="tpu_custom_call" | custom-call | tf_op jit(solution)/shard_map/while/body/product/pallas_call | solution.py:192
  127.2 3.6 %collective-permute-done = f32[12,16,2048]{2,1,0:T(8,128)S(1)} collective-permute-done((f32[12,16,2048]{2,1,0:T(8,128)}, f32[12,16,2048]{2,1,0:T(8,128)S(1)}, u32[]{:S(2)}, u32[]{:S(2)}) %collective-permute-start) | collective-permute-done | bytes 1572896 | tf_op jit(solution)/shard_map/while/body/ppermute | solution.py:214
  134.6 18.1 %collective-permute-done.1 = f32[12,2,4,2048]{3,2,0,1:T(4,128)S(1)} collective-permute-done((f32[12,2,4,2048]{3,2,0,1:T(4,128)S(1)}, f32[12,2,4,2048]{3,2,0,1:T(4,128)S(1)}, u32[]{:S(2)}, u32[]{:S(2)}) %collective-permute-start.1) | collective-permute-done | bytes 786464 | tf_op jit(solution)/shard_map/while/body/ppermute | solution.py:214
  154.6 8.9 %collective-permute-done.2 = f32[12,1,4,2048]{3,2,0,1:T(4,128)S(1)} collective-permute-done((f32[12,1,4,2048]{3,2,0,1:T(4,128)S(1)}, f32[12,1,4,2048]{3,2,0,1:T(4,128)S(1)}, u32[]{:S(2)}, u32[]{:S(2)}) %collective-permute-start.2) | collective-permute-done | bytes 393248 | tf_op jit(solution)/shard_map/while/body/ppermute | solution.py:214
  164.3 10.4 %collective-permute-done.8.refs_0_ = bf16[2,16,32,512]{3,2,1,0:T(8,128)(2,1)} collective-permute-done((bf16[2,16,32,512]{3,2,1,0:T(8,128)(2,1)}, bf16[2,16,32,512]{3,2,1,0:T(8,128)(2,1)}, u32[]{:S(2)}, u32[]{:S(2)}) %collective-permute-start.8) | collective-permute-done | bytes 1048608 | tf_op jit(solution)/shard_map/ppermute | solution.py:214
  174.8 16.6 %product.6 = (f32[4,16,2048]{2,1,0:T(8,128)}, f32[4,16,2048]{2,1,0:T(8,128)}) custom-call(s32[1]{0:T(128)} %bitcast.4.me_ref, bf16[2,16,32,512]{3,2,1,0:T(8,128)(2,1)} %collective-permute-done.8.refs_0_, bf16[2,16,32,512]{3,2,1,0:T(8,128)(2,1)} %collective-permute-done.9.refs_1_, bf16[16,2048,512]{2,1,0:T(8,128)(2,1)} %get-tuple-element.587, ...), custom_call_target="tpu_custom_call" | custom-call | tf_op jit(solution)/shard_map/product/pallas_call | solution.py:192
  191.4 2.1 collective-permute-done.10
  195.0 2.5 %collective-permute-start.13 = (f32[4,4,2048]{2,0,1:T(4,128)S(1)}, f32[4,4,2048]{2,0,1:T(4,128)S(1)}, u32[]{:S(2)}, u32[]{:S(2)}) collective-permute-start(f32[4,4,2048]{2,0,1:T(4,128)S(1)} %bitcast.77), channel_id=1, source_target_pairs={{0,24},{8,16},{16,8},{24,0},{1,25},{9,17},{17,9},{25,1},{2,26},{10... | collective-permute-start | bytes 393224 | tf_op jit(solution)/shard_map/ppermute | solution.py:214
  199.3 23.0 %collective-permute-start.5 = (f32[12,2048]{1,0:T(8,128)S(1)}, f32[12,2048]{1,0:T(8,128)S(1)}, u32[]{:S(2)}, u32[]{:S(2)}) collective-permute-start(f32[12,2048]{1,0:T(8,128)S(1)} %bitcast.75), channel_id=1, source_target_pairs={{0,2},{1,3},{2,0},{3,1},{4,6},{5,7},{6,4},{7,5},{8,10},{9,11},{10,... | collective-permute-start | bytes 294920 | tf_op jit(solution)/shard_map/ppermute | solution.py:214
  223.1 1.8 collective-permute-start.7
  225.7 2.4 collective-permute-start.14
  231.1 4.9 %collective-permute-done.6.refs_2_ = f32[12,2048]{1,0:T(8,128)S(1)} collective-permute-done((f32[12,2048]{1,0:T(8,128)S(1)}, f32[12,2048]{1,0:T(8,128)S(1)}, u32[]{:S(2)}, u32[]{:S(2)}) %collective-permute-start.6) | collective-permute-done | bytes 98336 | tf_op jit(solution)/shard_map/ppermute | solution.py:214
  236.0 2.6 %collective-permute-done.15.refs_6_ = f32[4,2048]{1,0:T(4,128)S(1)} collective-permute-done((f32[4,2048]{1,0:T(4,128)S(1)}, f32[4,2048]{1,0:T(4,128)S(1)}, u32[]{:S(2)}, u32[]{:S(2)}) %collective-permute-start.15) | collective-permute-done | bytes 32800 | tf_op jit(solution)/shard_map/ppermute | solution.py:214
  239.2 1.8 combine.1
  (63 shorter events, 19.0 us)
Async XLA Ops:
  4.3 100.5 %all-to-all-start = ((bf16[8,16,32,512]{3,2,1,0:T(8,128)(2,1)}), bf16[8,16,32,512]{3,2,1,0:T(8,128)(2,1)}, u32[]{:S(2)}, u32[]{:S(2)}) async-start(bf16[8,16,32,512]{3,2,1,0:T(8,128)(2,1)} %screen.1), calls=%async_computation | async-start | bytes 8388608 | tf_op jit(solution)/shard_map/all_to_all | solution.py:287
  39.7 4.5 %collective-permute-start.3 = (bf16[4,16,32,512]{3,2,1,0:T(8,128)(2,1)}, bf16[4,16,32,512]{3,2,1,0:T(8,128)(2,1)S(1)}, u32[]{:S(2)}, u32[]{:S(2)}) collective-permute-start(bf16[4,16,32,512]{3,2,1,0:T(8,128)(2,1)} %give.1), channel_id=1, source_target_pairs={{0,1},{1,0},{2,3},{3,2},{4,5},{5,4},{6,7},{7,6},{8,9},{9,8},{10,11... | collective-permute-start | bytes 6291464 | tf_op jit(solution)/shard_map/ppermute | solution.py:214
  48.3 57.8 %collective-permute-start.4 = (bf16[2,16,32,512]{3,2,1,0:T(8,128)(2,1)}, bf16[2,16,32,512]{3,2,1,0:T(8,128)(2,1)}, u32[]{:S(2)}, u32[]{:S(2)}) collective-permute-start(bf16[2,16,32,512]{3,2,1,0:T(8,128)(2,1)} %get-tuple-element.427), channel_id=1, source_target_pairs={{0,2},{1,3},{2,0},{3,1},{4,6},{5,7},{6,4},{7,5},{8,10},{9,11},{10,... | collective-permute-start | bytes 3145736 | tf_op jit(solution)/shard_map/ppermute | solution.py:214
  104.7 70.0 %collective-permute-start.8 = (bf16[2,16,32,512]{3,2,1,0:T(8,128)(2,1)}, bf16[2,16,32,512]{3,2,1,0:T(8,128)(2,1)}, u32[]{:S(2)}, u32[]{:S(2)}) collective-permute-start(bf16[2,16,32,512]{3,2,1,0:T(8,128)(2,1)} %get-tuple-element.431), channel_id=1, source_target_pairs={{0,4},{1,5},{2,6},{3,7},{4,0},{5,1},{6,2},{7,3},{8,12},{9,13},{10,... | collective-permute-start | bytes 3145736 | tf_op jit(solution)/shard_map/ppermute | solution.py:214
  104.7 70.0 %collective-permute-start.9 = (bf16[2,16,32,512]{3,2,1,0:T(8,128)(2,1)}, bf16[2,16,32,512]{3,2,1,0:T(8,128)(2,1)}, u32[]{:S(2)}, u32[]{:S(2)}) collective-permute-start(bf16[2,16,32,512]{3,2,1,0:T(8,128)(2,1)} %get-tuple-element.432), channel_id=1, source_target_pairs={{0,6},{1,7},{2,4},{3,5},{4,2},{5,3},{6,0},{7,1},{8,14},{9,15},{10,... | collective-permute-start | bytes 3145736 | tf_op jit(solution)/shard_map/ppermute | solution.py:214
  106.9 20.3 %copy-start.1 = (bf16[2,16,32,512]{3,2,1,0:T(8,128)(2,1)}, bf16[2,16,32,512]{3,2,1,0:T(8,128)(2,1)S(1)}, u32[]{:S(2)}) copy-start(bf16[2,16,32,512]{3,2,1,0:T(8,128)(2,1)S(1)} %get-tuple-element.577.refs_1_) | copy-start | bytes 3145732 | tf_op jit(solution)/shard_map/while
  127.2 3.6 %collective-permute-start = (f32[12,16,2048]{2,1,0:T(8,128)}, f32[12,16,2048]{2,1,0:T(8,128)S(1)}, u32[]{:S(2)}, u32[]{:S(2)}) collective-permute-start(f32[12,16,2048]{2,1,0:T(8,128)} %get-tuple-element.542), channel_id=1, source_target_pairs={{0,1},{1,0},{2,3},{3,2},{4,5},{5,4},{6,7},{7,6},{8,9},{9,8},{10,11... | collective-permute-start | bytes 4718600 | tf_op jit(solution)/shard_map/while/body/ppermute | solution.py:214
  133.1 19.6 %collective-permute-start.1 = (f32[12,2,4,2048]{3,2,0,1:T(4,128)S(1)}, f32[12,2,4,2048]{3,2,0,1:T(4,128)S(1)}, u32[]{:S(2)}, u32[]{:S(2)}) collective-permute-start(f32[12,2,4,2048]{3,2,0,1:T(4,128)S(1)} %bitcast.71), channel_id=1, source_target_pairs={{0,8},{8,0},{16,24},{24,16},{1,9},{9,1},{17,25},{25,17},{2,10},{10... | collective-permute-start | bytes 2359304 | tf_op jit(solution)/shard_map/while/body/ppermute | solution.py:214
  152.7 11.6 %copy-start.2 = (bf16[2,16,32,512]{3,2,1,0:T(8,128)(2,1)S(1)}, bf16[2,16,32,512]{3,2,1,0:T(8,128)(2,1)}, u32[]{:S(2)}) copy-start(bf16[2,16,32,512]{3,2,1,0:T(8,128)(2,1)} %copy-done.1) | copy-start | bytes 3145732 | tf_op jit(solution)/shard_map/while
  153.0 10.5 %collective-permute-start.2 = (f32[12,1,4,2048]{3,2,0,1:T(4,128)S(1)}, f32[12,1,4,2048]{3,2,0,1:T(4,128)S(1)}, u32[]{:S(2)}, u32[]{:S(2)}) collective-permute-start(f32[12,1,4,2048]{3,2,0,1:T(4,128)S(1)} %constant_dynamic-slice_fusion.14), channel_id=1, source_target_pairs={{0,16},{8,24},{16,0},{24,8},{1,17},{9,25},{17,1},{25,9},{2,18},{10... | collective-permute-start | bytes 1179656 | tf_op jit(solution)/shard_map/while/body/ppermute | solution.py:214
  191.4 2.1 collective-permute-start.10
  193.5 5.3 %copy-start.3 = (f32[12,4,2048]{2,1,0:T(4,128)S(1)}, f32[12,4,2048]{2,1,0:T(4,128)}, u32[]{:S(2)}) copy-start(f32[12,4,2048]{2,1,0:T(4,128)} %get-tuple-element.428.refs_3_) | copy-start | bytes 1179652
  195.0 28.1 %collective-permute-start.13 = (f32[4,4,2048]{2,0,1:T(4,128)S(1)}, f32[4,4,2048]{2,0,1:T(4,128)S(1)}, u32[]{:S(2)}, u32[]{:S(2)}) collective-permute-start(f32[4,4,2048]{2,0,1:T(4,128)S(1)} %bitcast.77), channel_id=1, source_target_pairs={{0,24},{8,16},{16,8},{24,0},{1,25},{9,17},{17,9},{25,1},{2,26},{10... | collective-permute-start | bytes 393224 | tf_op jit(solution)/shard_map/ppermute | solution.py:214
  197.6 27.3 %collective-permute-start.12 = (f32[4,4,2048]{2,0,1:T(4,128)S(1)}, f32[4,4,2048]{2,0,1:T(4,128)S(1)}, u32[]{:S(2)}, u32[]{:S(2)}) collective-permute-start(f32[4,4,2048]{2,0,1:T(4,128)S(1)} %bitcast.76), channel_id=1, source_target_pairs={{0,16},{8,24},{16,0},{24,8},{1,17},{9,25},{17,1},{25,9},{2,18},{10... | collective-permute-start | bytes 393224 | tf_op jit(solution)/shard_map/ppermute | solution.py:214
  198.3 26.6 %collective-permute-start.11 = (f32[4,4,2048]{2,0,1:T(4,128)S(1)}, f32[4,4,2048]{2,0,1:T(4,128)S(1)}, u32[]{:S(2)}, u32[]{:S(2)}) collective-permute-start(f32[4,4,2048]{2,0,1:T(4,128)S(1)} %bitcast.78), channel_id=1, source_target_pairs={{0,8},{8,0},{16,24},{24,16},{1,9},{9,1},{17,25},{25,17},{2,10},{10... | collective-permute-start | bytes 393224 | tf_op jit(solution)/shard_map/ppermute | solution.py:214
  199.3 29.4 %collective-permute-start.5 = (f32[12,2048]{1,0:T(8,128)S(1)}, f32[12,2048]{1,0:T(8,128)S(1)}, u32[]{:S(2)}, u32[]{:S(2)}) collective-permute-start(f32[12,2048]{1,0:T(8,128)S(1)} %bitcast.75), channel_id=1, source_target_pairs={{0,2},{1,3},{2,0},{3,1},{4,6},{5,7},{6,4},{7,5},{8,10},{9,11},{10,... | collective-permute-start | bytes 294920 | tf_op jit(solution)/shard_map/ppermute | solution.py:214
  222.3 13.6 %collective-permute-start.6 = (f32[12,2048]{1,0:T(8,128)S(1)}, f32[12,2048]{1,0:T(8,128)S(1)}, u32[]{:S(2)}, u32[]{:S(2)}) collective-permute-start(f32[12,2048]{1,0:T(8,128)S(1)} %bitcast.73), channel_id=1, source_target_pairs={{0,4},{1,5},{2,6},{3,7},{4,0},{5,1},{6,2},{7,3},{8,12},{9,13},{10,... | collective-permute-start | bytes 294920 | tf_op jit(solution)/shard_map/ppermute | solution.py:214
  223.1 12.9 %collective-permute-start.7 = (f32[12,2048]{1,0:T(8,128)S(1)}, f32[12,2048]{1,0:T(8,128)S(1)}, u32[]{:S(2)}, u32[]{:S(2)}) collective-permute-start(f32[12,2048]{1,0:T(8,128)S(1)} %bitcast.74), channel_id=1, source_target_pairs={{0,6},{1,7},{2,4},{3,5},{4,2},{5,3},{6,0},{7,1},{8,14},{9,15},{10,... | collective-permute-start | bytes 294920 | tf_op jit(solution)/shard_map/ppermute | solution.py:214
  225.7 10.3 %collective-permute-start.14 = (f32[4,2048]{1,0:T(4,128)S(1)}, f32[4,2048]{1,0:T(4,128)S(1)}, u32[]{:S(2)}, u32[]{:S(2)}) collective-permute-start(f32[4,2048]{1,0:T(4,128)S(1)} %get-tuple-element.469), channel_id=1, source_target_pairs={{0,2},{1,3},{2,0},{3,1},{4,6},{5,7},{6,4},{7,5},{8,10},{9,11},{10,... | collective-permute-start | bytes 98312 | tf_op jit(solution)/shard_map/ppermute | solution.py:214
  228.0 10.6 %collective-permute-start.15 = (f32[4,2048]{1,0:T(4,128)S(1)}, f32[4,2048]{1,0:T(4,128)S(1)}, u32[]{:S(2)}, u32[]{:S(2)}) collective-permute-start(f32[4,2048]{1,0:T(4,128)S(1)} %get-tuple-element.468), channel_id=1, source_target_pairs={{0,4},{1,5},{2,6},{3,7},{4,0},{5,1},{6,2},{7,3},{8,12},{9,13},{10,... | collective-permute-start | bytes 98312 | tf_op jit(solution)/shard_map/ppermute | solution.py:214
  228.7 9.9 %copy-start.4 = (f32[12,2048]{1,0:T(8,128)}, f32[12,2048]{1,0:T(8,128)S(1)}, u32[]{:S(2)}) copy-start(f32[12,2048]{1,0:T(8,128)S(1)} %collective-permute-done.5.refs_1_) | copy-start | bytes 294916
  228.7 9.9 %collective-permute-start.16 = (f32[4,2048]{1,0:T(4,128)S(1)}, f32[4,2048]{1,0:T(4,128)S(1)}, u32[]{:S(2)}, u32[]{:S(2)}) collective-permute-start(f32[4,2048]{1,0:T(4,128)S(1)} %get-tuple-element.467), channel_id=1, source_target_pairs={{0,6},{1,7},{2,4},{3,5},{4,2},{5,3},{6,0},{7,1},{8,14},{9,15},{10,... | collective-permute-start | bytes 98312 | tf_op jit(solution)/shard_map/ppermute | solution.py:214
  236.0 2.6 %copy-start.6 = (f32[12,2048]{1,0:T(8,128)}, f32[12,2048]{1,0:T(8,128)S(1)}, u32[]{:S(2)}) copy-start(f32[12,2048]{1,0:T(8,128)S(1)} %collective-permute-done.7.refs_3_) | copy-start | bytes 294916
  236.0 2.6 %copy-start.7 = (f32[4,2048]{1,0:T(4,128)}, f32[4,2048]{1,0:T(4,128)S(1)}, u32[]{:S(2)}) copy-start(f32[4,2048]{1,0:T(4,128)S(1)} %collective-permute-done.14.refs_5_) | copy-start | bytes 98308
  (4 other events, 5.3 us)

commit v4 on v3

--- a/solution.py
+++ b/solution.py
@@ -9,6 +9,7 @@
 
 TILE = 64
 VMEM = 60 << 20
+HELD = 12 << 20
 
 
 def screen_block(amp, screen_ref, dest):
@@ -206,6 +207,69 @@
     )(position() + 2 * turn, *lefts, weights, *after)
 
 
+def hold_kernel(weight_ref, *refs):
+    out_ref, sems = refs[-2:]
+    copies = [
+        pltpu.make_async_copy(weight_ref.at[k], out_ref.at[k], sems.at[k]) for k in range(weight_ref.shape[0])
+    ]
+    for copy in copies:
+        copy.start()
+    for copy in copies:
+        copy.wait()
+
+
+def held_in_vmem(weights, after):
+    return pl.pallas_call(
+        hold_kernel,
+        in_specs=[pl.BlockSpec(memory_space=pl.ANY)] * (1 + len(after)),
+        out_specs=pl.BlockSpec(memory_space=pltpu.VMEM),
+        out_shape=pltpu.VMEM(weights.shape, weights.dtype),
+        scratch_shapes=[pltpu.SemaphoreType.DMA((weights.shape[0],))],
+        compiler_params=pltpu.CompilerParams(vmem_limit_bytes=1 << 20),
+        cost_estimate=pl.CostEstimate(flops=0, bytes_accessed=0, transcendentals=0),
+        name="hold",
+    )(weights, *after)
+
+
+def held_product_kernel(*refs, block, turned):
+    *left_refs, weight_ref, mine_ref, give_ref = refs
+    piece, columns = mine_ref.shape[1:]
+    odd = lax.axis_index("vir") % 2 == 1
+
+    @pl.loop(0, columns // block)
+    def _(n):
+        at = pl.multiple_of(n * block, block)
+        total = None
+        for k in range(weight_ref.shape[0]):
+            left = jnp.concatenate([ref[unit, k] for ref in left_refs for unit in range(ref.shape[0])], axis=0)
+            weight = weight_ref[k, pl.ds(at, block)]
+            term = lax.dot_general(
+                *((weight, left) if turned else (left, weight)),
+                (((1,), (1,)), ((), ())),
+                preferred_element_type=jnp.float32,
+            )
+            total = term if total is None else total + term
+        if turned:
+            total = total.T
+        for unit in range(mine_ref.shape[0]):
+            zero, one = (total[(2 * unit + core) * piece : (2 * unit + core + 1) * piece] for core in range(2))
+            mine_ref[unit, :, pl.ds(at, block)] = jnp.where(odd, one, zero)
+            give_ref[unit ^ 1, :, pl.ds(at, block)] = jnp.where(odd, zero, one)
+
+
+def held_product(lefts, weights, block, turned):
+    shape = (sum(x.shape[0] for x in lefts), lefts[0].shape[2] // 2, weights.shape[1])
+    return pl.pallas_call(
+        functools.partial(held_product_kernel, block=block, turned=turned),
+        in_specs=[pl.BlockSpec(memory_space=pltpu.VMEM)] * (1 + len(lefts)),
+        out_specs=[pl.BlockSpec(memory_space=pltpu.VMEM)] * 2,
+        out_shape=[jax.ShapeDtypeStruct(shape, jnp.float32)] * 2,
+        compiler_params=pltpu.CompilerParams(vmem_limit_bytes=HELD),
+        cost_estimate=pl.CostEstimate(flops=0, bytes_accessed=0, transcendentals=0),
+        name="product_held",
+    )(*lefts, weights)
+
+
 def pick(x, at, axis):
     return lax.dynamic_index_in_dim(x, at, axis, keepdims=False)
 
@@ -301,9 +365,11 @@
     once = 1 + lax.axis_index("vir") // n_vir
     units = n_vir + 2 * len(soon)
     early_sums = lax.fori_loop(0, once, early, jnp.zeros((units, n_z, columns), jnp.float32))
-    mine, give = product(last[len(soon) :], weights, 512, 0, after=(early_sums,))
+    mine, give = held_product(last[len(soon) :], held_in_vmem(weights, (early_sums,)), 512, True)
+    early_terms = along_z(early_sums, n_vir)
+    [give] = held_back([give], early_terms[:2])
     late_sums = over_plane(over_cores(mine, give, n_occ, n_vir), n_occ)
-    return combined(along_z(early_sums, n_vir), along_z(late_sums, n_vir))
+    return combined(early_terms, along_z(late_sums, n_vir))
 
 
 def on_any(amplitudes, integrals, screen):

time: 242 us -> 233 us (0.963)
  waiting for transfers between devices: 106 us -> 95 us
  starting transfers between devices: 47.2 us -> 38.3 us
  local copies, waits for them, and re-layouts: 28.5 us -> 35.9 us
  Pallas kernels: 55 us -> 58.8 us
    pallas_call x0 -> x2, Pallas kernels: none -> 20.3 us  [the longest x1 10.8 us: held_in_vmem(): pl.pallas_call(hold_kernel, in_specs=[pl.BlockSpec(memory_space=pl.ANY)]...]
    pallas_call x2 -> x1, Pallas kernels: 36.9 us -> 20.3 us  [product(): pl.pallas_call(functools.partial(product_kernel, count=len(lefts), plain=...]
    ppermute x17, waiting for transfers between devices: 54.7 us -> 43.5 us  [exchange(): return lax.ppermute(x, axis_name, [(j, j ^ step) for j in range(size)])]
    ppermute x17, starting transfers between devices: 40.8 us -> 32 us  [exchange(): return lax.ppermute(x, axis_name, [(j, j ^ step) for j in range(size)])]
    dynamic_slice x7, local copies, waits for them, and re-layouts: 0.9 us -> 3.94 us  [pick(): return lax.dynamic_index_in_dim(x, at, axis, keepdims=False)]
  transfers between devices with their start and end apart: 18 -> 18, of which waited for: 9 -> 8; matrix products, arithmetic and copies ran while one was open for 12% -> 16% of each run, Pallas kernels for 13% -> 23%
where the time goes in v4:
time: 233 us; the launch traced here: 232 us
  waiting for transfers between devices  95 us (41%)
  Pallas kernels  58.8 us (25%)
  starting transfers between devices  38.3 us (16%)
  local copies, waits for them, and re-layouts  35.9 us (15%)
  other arithmetic  4.01 us (2%)
    all_to_all x1, waiting for transfers between devices, on_block(): lax.all_to_all(screened(amplitudes, screen, n_occ, n_vir), 'vir', 0, 0, t...  51.5 us
    ppermute x17, waiting for transfers between devices, exchange(): return lax.ppermute(x, axis_name, [(j, j ^ step) for j in range(size)])  43.5 us
    ppermute x17, starting transfers between devices, exchange(): return lax.ppermute(x, axis_name, [(j, j ^ step) for j in range(size)])  32 us
    unnamed x21, local copies, waits for them, and re-layouts  26.9 us
    pallas_call x1, Pallas kernels, product(): pl.pallas_call(functools.partial(product_kernel, count=len(lefts), plain=...  20.3 us
    pallas_call x1, Pallas kernels, held_in_vmem(): pl.pallas_call(hold_kernel, in_specs=[pl.BlockSpec(memory_space=pl.ANY)]...  10.8 us
    pallas_call x1, Pallas kernels, held_product(): pl.pallas_call(functools.partial(held_product_kernel, block=block, turned...  9.55 us
    pallas_call x1, Pallas kernels, given(): pl.pallas_call(functools.partial(give_kernel, steps=steps), grid_spec=plt...  6.39 us
  transfers between devices with their start and end apart: 18, of which 8 were waited for; matrix products, arithmetic and copies ran while one was open for 16% of the time, Pallas kernels for 23%

profile of v4, /device:TPU:0, one launch (start us, length us, event | category | flops | bytes accessed | tf_op | source)
XLA Modules:
  0.0 232.3 jit_solution(14222022371369147188)
XLA Ops:
  0.0 4.3 %screen.1 = bf16[8,16,32,512]{3,2,1,0:T(8,128)(2,1)} custom-call(bf16[4,4,2,2,16,4096]{5,4,3,2,1,0:T(8,128)(2,1)} %bitcast.58, bf16[4,4,2,2,16,4096]{5,4,3,2,1,0:T(8,128)(2,1)} %bitcast.59, bf16[4,4,2,2,16,4096]{5,4,3,2,1,0:T(8,128)(2,1)} %bitcast.60, bf16[4,4,2,2,16,4096]{5,4,3,2,1,0:T(8,128)(2,1)} %bitcast.61, bf16[4,4,2,2,16,4096]{5,4,3,2,1,0:T(8,128)(2,1)} %bitcast.62, ...), custom_call_target="tpu_custom_call" | custom-call | tf_op jit(solution)/shard_map/screen/pallas_call | solution.py:140
  4.3 6.3 %all-to-all-start = ((bf16[8,16,32,512]{3,2,1,0:T(8,128)(2,1)}), bf16[8,16,32,512]{3,2,1,0:T(8,128)(2,1)}, u32[]{:S(2)}, u32[]{:S(2)}) async-start(bf16[8,16,32,512]{3,2,1,0:T(8,128)(2,1)} %screen.1), calls=%async_computation | async-start | bytes 8388608 | tf_op jit(solution)/shard_map/all_to_all | solution.py:351
  10.6 22.7 %copy.9 = bf16[64,32,16,512]{3,1,0,2:T(8,128)(2,1)} copy(bf16[64,32,16,512]{3,2,1,0:T(8,128)(2,1)} %param.6) | data formatting | bytes 67108864 | tf_op args[1]
  33.3 6.4 %give.1 = bf16[4,16,32,512]{3,2,1,0:T(8,128)(2,1)} custom-call(s32[1]{0:T(128)} %bitcast.4.me_ref, bf16[4,4,2,2,16,4096]{5,4,3,2,1,0:T(8,128)(2,1)} %bitcast.66, s32[1,16,64]{2,1,0:T(8,128)} %refs_2_.3, bf16[16,2048,512]{2,1,0:T(8,128)(2,1)} %bitcast.56), custom_call_target="tpu_custom_call" | custom-call | tf_op jit(solution)/shard_map/give/pallas_call | solution.py:61
  40.2 4.0 %collective-permute-done.3.refs_3_.refs_4_ = bf16[4,16,32,512]{3,2,1,0:T(8,128)(2,1)S(1)} collective-permute-done((bf16[4,16,32,512]{3,2,1,0:T(8,128)(2,1)}, bf16[4,16,32,512]{3,2,1,0:T(8,128)(2,1)S(1)}, u32[]{:S(2)}, u32[]{:S(2)}) %collective-permute-start.3) | collective-permute-done | bytes 2097184 | tf_op jit(solution)/shard_map/ppermute | solution.py:278
  45.5 2.9 %keep.2 = (bf16[2,16,32,512]{3,2,1,0:T(8,128)(2,1)}, bf16[2,16,32,512]{3,2,1,0:T(8,128)(2,1)}) custom-call(s32[1]{0:T(128)} %bitcast.4.me_ref, bf16[4,4,2,2,16,4096]{5,4,3,2,1,0:T(8,128)(2,1)} %bitcast.67, bf16[4,4,2,2,16,4096]{5,4,3,2,1,0:T(8,128)(2,1)} %bitcast.68, s32[1,16,64]{2,1,0:T(8,128)} %refs_2_.3, bf16[4,16,32,512]{3,2,1,0:T(8,128)(2,1)} %copy-done.1, ...), custom_call_target="tpu_custom_call" | custom-call | tf_op jit(solution)/shard_map/keep/pallas_call | solution.py:96
  50.3 2.9 %keep.3 = (bf16[2,16,32,512]{3,2,1,0:T(8,128)(2,1)}, bf16[2,16,32,512]{3,2,1,0:T(8,128)(2,1)}) custom-call(s32[1]{0:T(128)} %bitcast.4.me_ref, bf16[4,4,2,2,16,4096]{5,4,3,2,1,0:T(8,128)(2,1)} %bitcast.69, bf16[4,4,2,2,16,4096]{5,4,3,2,1,0:T(8,128)(2,1)} %bitcast.70, s32[1,16,64]{2,1,0:T(8,128)} %refs_2_.3, bf16[4,16,32,512]{3,2,1,0:T(8,128)(2,1)} %copy-done.1, ...), custom_call_target="tpu_custom_call" | custom-call | tf_op jit(solution)/shard_map/keep/pallas_call | solution.py:96
  53.2 51.5 %all-to-all-done.refs_2_ = bf16[8,16,32,512]{3,2,1,0:T(8,128)(2,1)} async-done(((bf16[8,16,32,512]{3,2,1,0:T(8,128)(2,1)}), bf16[8,16,32,512]{3,2,1,0:T(8,128)(2,1)}, u32[]{:S(2)}, u32[]{:S(2)}) %all-to-all-start) | async-done | bytes 4194336 | tf_op jit(solution)/shard_map/all_to_all | solution.py:351
  106.9 63.0 %while.14 = (s32[]{:T(128)}, f32[12,4,2048]{2,1,0:T(4,128)}, s32[]{:T(128)}, bf16[8,16,32,512]{3,2,1,0:T(8,128)(2,1)}, bf16[2,16,32,512]{3,2,1,0:T(8,128)(2,1)},...) while((s32[]{:T(128)}, f32[12,4,2048]{2,1,0:T(4,128)}, ...), condition=%wide.region_1.2_spmd, body=%wide.region_0.1_spmd.sunk | while | flops 688134 | bytes 27918648 | solution.py:367
  106.9 20.3 %product.5 = (f32[12,16,2048]{2,1,0:T(8,128)}, f32[12,16,2048]{2,1,0:T(8,128)}) custom-call(s32[1]{0:T(128)} %bitcast.54.me_ref, bf16[8,16,32,512]{3,2,1,0:T(8,128)(2,1)} %get-tuple-element.576.refs_0_, bf16[2,16,32,512]{3,2,1,0:T(8,128)(2,1)} %get-tuple-element.577.refs_1_, bf16[2,16,32,512]{3,2,1,0:T(8,128)(2,1)} %get-tuple-element.578.refs_2_, ...), custom_call_target="tpu_custom_call" | custom-call | tf_op jit(solution)/shard_map/while/body/product/pallas_call | solution.py:193
  127.2 3.6 %collective-permute-done = f32[12,16,2048]{2,1,0:T(8,128)S(1)} collective-permute-done((f32[12,16,2048]{2,1,0:T(8,128)}, f32[12,16,2048]{2,1,0:T(8,128)S(1)}, u32[]{:S(2)}, u32[]{:S(2)}) %collective-permute-start) | collective-permute-done | bytes 1572896 | tf_op jit(solution)/shard_map/while/body/ppermute | solution.py:278
  130.8 2.7 %add.166 = f32[12,16,2048]{2,1,0:T(8,128)} add(f32[12,16,2048]{2,1,0:T(8,128)} %get-tuple-element.541, f32[12,16,2048]{2,1,0:T(8,128)S(1)} %collective-permute-done) | non-fusion elementwise | flops 393216 | bytes 4718592 | tf_op jit(solution)/shard_map/while/body/add | solution.py:282
  133.6 2.7 %reshape.41 = f32[12,2,2,4,2048]{4,3,2,1,0:T(4,128)} reshape(f32[12,16,2048]{2,1,0:T(8,128)} %add.166) | data formatting | bytes 3145728 | tf_op jit(solution)/shard_map/while/body/reshape;while/body/reshape | solution.py:298
  139.4 18.1 %collective-permute-done.1 = f32[12,2,4,2048]{3,2,0,1:T(4,128)S(1)} collective-permute-done((f32[12,2,4,2048]{3,2,0,1:T(4,128)S(1)}, f32[12,2,4,2048]{3,2,0,1:T(4,128)S(1)}, u32[]{:S(2)}, u32[]{:S(2)}) %collective-permute-start.1) | collective-permute-done | bytes 786464 | tf_op jit(solution)/shard_map/while/body/ppermute | solution.py:278
  160.1 9.0 %collective-permute-done.2 = f32[12,1,4,2048]{3,2,0,1:T(4,128)S(1)} collective-permute-done((f32[12,1,4,2048]{3,2,0,1:T(4,128)}, f32[12,1,4,2048]{3,2,0,1:T(4,128)S(1)}, u32[]{:S(2)}, u32[]{:S(2)}) %collective-permute-start.2) | collective-permute-done | bytes 393248 | tf_op jit(solution)/shard_map/while/body/ppermute | solution.py:278
  172.0 2.2 collective-permute-start.5
  174.2 10.8 %hold.1.refs_2_ = bf16[16,2048,512]{2,1,0:T(8,128)(2,1)S(1)} custom-call(bf16[16,2048,512]{2,1,0:T(8,128)(2,1)} %get-tuple-element.590, f32[12,4,2048]{2,1,0:T(4,128)} %get-tuple-element.428.refs_0_), custom_call_target="tpu_custom_call" | custom-call | tf_op jit(solution)/shard_map/hold/pallas_call | solution.py:222
  185.7 9.5 %product_held.1 = (f32[4,16,2048]{2,1,0:T(8,128)S(1)}, f32[4,16,2048]{2,1,0:T(8,128)S(1)}) custom-call(bf16[2,16,32,512]{3,2,1,0:T(8,128)(2,1)S(1)} %collective-permute-done.8.refs_0_, bf16[2,16,32,512]{3,2,1,0:T(8,128)(2,1)S(1)} %collective-permute-done.9.refs_1_, bf16[16,2048,512]{2,1,0:T(8,128)(2,1)S(1)} %hold.1.refs_2_), custom_call_target="tpu_custom_call" | custom-call | tf_op jit(solution)/shard_map/product_held/pallas_call | solution.py:262
  196.7 2.1 collective-permute-done.10
  203.0 12.6 %collective-permute-start.6 = (f32[12,2048]{1,0:T(8,128)S(1)}, f32[12,2048]{1,0:T(8,128)S(1)}, u32[]{:S(2)}, u32[]{:S(2)}) collective-permute-start(f32[12,2048]{1,0:T(8,128)S(1)} %bitcast.75), channel_id=1, source_target_pairs={{0,4},{1,5},{2,6},{3,7},{4,0},{5,1},{6,2},{7,3},{8,12},{9,13},{10,... | collective-permute-start | bytes 294920 | tf_op jit(solution)/shard_map/ppermute | solution.py:278
  218.1 2.1 collective-permute-start.16
  220.2 2.9 %collective-permute-start.15 = (f32[4,2048]{1,0:T(4,128)S(1)}, f32[4,2048]{1,0:T(4,128)S(1)}, u32[]{:S(2)}, u32[]{:S(2)}) collective-permute-start(f32[4,2048]{1,0:T(4,128)S(1)} %get-tuple-element.468), channel_id=1, source_target_pairs={{0,4},{1,5},{2,6},{3,7},{4,0},{5,1},{6,2},{7,3},{8,12},{9,13},{10,... | collective-permute-start | bytes 98312 | tf_op jit(solution)/shard_map/ppermute | solution.py:278
  223.1 3.5 %collective-permute-done.6.refs_2_ = f32[12,2048]{1,0:T(8,128)S(1)} collective-permute-done((f32[12,2048]{1,0:T(8,128)S(1)}, f32[12,2048]{1,0:T(8,128)S(1)}, u32[]{:S(2)}, u32[]{:S(2)}) %collective-permute-start.6) | collective-permute-done | bytes 98336 | tf_op jit(solution)/shard_map/ppermute | solution.py:278
  226.7 3.1 %collective-permute-done.15.refs_6_ = f32[4,2048]{1,0:T(4,128)S(1)} collective-permute-done((f32[4,2048]{1,0:T(4,128)S(1)}, f32[4,2048]{1,0:T(4,128)S(1)}, u32[]{:S(2)}, u32[]{:S(2)}) %collective-permute-start.15) | collective-permute-done | bytes 32800 | tf_op jit(solution)/shard_map/ppermute | solution.py:278
  (61 shorter events, 25.8 us)
Async XLA Ops:
  4.3 100.5 %all-to-all-start = ((bf16[8,16,32,512]{3,2,1,0:T(8,128)(2,1)}), bf16[8,16,32,512]{3,2,1,0:T(8,128)(2,1)}, u32[]{:S(2)}, u32[]{:S(2)}) async-start(bf16[8,16,32,512]{3,2,1,0:T(8,128)(2,1)} %screen.1), calls=%async_computation | async-start | bytes 8388608 | tf_op jit(solution)/shard_map/all_to_all | solution.py:351
  39.7 4.5 %collective-permute-start.3 = (bf16[4,16,32,512]{3,2,1,0:T(8,128)(2,1)}, bf16[4,16,32,512]{3,2,1,0:T(8,128)(2,1)S(1)}, u32[]{:S(2)}, u32[]{:S(2)}) collective-permute-start(bf16[4,16,32,512]{3,2,1,0:T(8,128)(2,1)} %give.1), channel_id=1, source_target_pairs={{0,1},{1,0},{2,3},{3,2},{4,5},{5,4},{6,7},{7,6},{8,9},{9,8},{10,11... | collective-permute-start | bytes 6291464 | tf_op jit(solution)/shard_map/ppermute | solution.py:278
  44.2 1.3 copy-start.1
  48.4 57.7 %collective-permute-start.4 = (bf16[2,16,32,512]{3,2,1,0:T(8,128)(2,1)}, bf16[2,16,32,512]{3,2,1,0:T(8,128)(2,1)}, u32[]{:S(2)}, u32[]{:S(2)}) collective-permute-start(bf16[2,16,32,512]{3,2,1,0:T(8,128)(2,1)} %get-tuple-element.427), channel_id=1, source_target_pairs={{0,2},{1,3},{2,0},{3,1},{4,6},{5,7},{6,4},{7,5},{8,10},{9,11},{10,... | collective-permute-start | bytes 3145736 | tf_op jit(solution)/shard_map/ppermute | solution.py:278
  104.7 80.9 %collective-permute-start.8 = (bf16[2,16,32,512]{3,2,1,0:T(8,128)(2,1)}, bf16[2,16,32,512]{3,2,1,0:T(8,128)(2,1)S(1)}, u32[]{:S(2)}, u32[]{:S(2)}) collective-permute-start(bf16[2,16,32,512]{3,2,1,0:T(8,128)(2,1)} %get-tuple-element.431), channel_id=1, source_target_pairs={{0,4},{1,5},{2,6},{3,7},{4,0},{5,1},{6,2},{7,3},{8,12},{9,13},{10,... | collective-permute-start | bytes 3145736 | tf_op jit(solution)/shard_map/ppermute | solution.py:278
  104.7 80.9 %collective-permute-start.9 = (bf16[2,16,32,512]{3,2,1,0:T(8,128)(2,1)}, bf16[2,16,32,512]{3,2,1,0:T(8,128)(2,1)S(1)}, u32[]{:S(2)}, u32[]{:S(2)}) collective-permute-start(bf16[2,16,32,512]{3,2,1,0:T(8,128)(2,1)} %get-tuple-element.432), channel_id=1, source_target_pairs={{0,6},{1,7},{2,4},{3,5},{4,2},{5,3},{6,0},{7,1},{8,14},{9,15},{10,... | collective-permute-start | bytes 3145736 | tf_op jit(solution)/shard_map/ppermute | solution.py:278
  127.2 3.6 %collective-permute-start = (f32[12,16,2048]{2,1,0:T(8,128)}, f32[12,16,2048]{2,1,0:T(8,128)S(1)}, u32[]{:S(2)}, u32[]{:S(2)}) collective-permute-start(f32[12,16,2048]{2,1,0:T(8,128)} %get-tuple-element.542), channel_id=1, source_target_pairs={{0,1},{1,0},{2,3},{3,2},{4,5},{5,4},{6,7},{7,6},{8,9},{9,8},{10,11... | collective-permute-start | bytes 4718600 | tf_op jit(solution)/shard_map/while/body/ppermute | solution.py:278
  137.9 19.6 %collective-permute-start.1 = (f32[12,2,4,2048]{3,2,0,1:T(4,128)S(1)}, f32[12,2,4,2048]{3,2,0,1:T(4,128)S(1)}, u32[]{:S(2)}, u32[]{:S(2)}) collective-permute-start(f32[12,2,4,2048]{3,2,0,1:T(4,128)S(1)} %bitcast.71), channel_id=1, source_target_pairs={{0,8},{8,0},{16,24},{24,16},{1,9},{9,1},{17,25},{25,17},{2,10},{10... | collective-permute-start | bytes 2359304 | tf_op jit(solution)/shard_map/while/body/ppermute | solution.py:278
  158.5 10.5 %collective-permute-start.2 = (f32[12,1,4,2048]{3,2,0,1:T(4,128)}, f32[12,1,4,2048]{3,2,0,1:T(4,128)S(1)}, u32[]{:S(2)}, u32[]{:S(2)}) collective-permute-start(f32[12,1,4,2048]{3,2,0,1:T(4,128)} %constant_dynamic-slice_fusion.14), channel_id=1, source_target_pairs={{0,16},{8,24},{16,0},{24,8},{1,17},{9,25},{17,1},{25,9},{2,18},{10... | collective-permute-start | bytes 1179656 | tf_op jit(solution)/shard_map/while/body/ppermute | solution.py:278
  172.0 24.0 %collective-permute-start.5 = (f32[12,2048]{1,0:T(8,128)S(1)}, f32[12,2048]{1,0:T(8,128)S(1)}, u32[]{:S(2)}, u32[]{:S(2)}) collective-permute-start(f32[12,2048]{1,0:T(8,128)S(1)} %bitcast.76), channel_id=1, source_target_pairs={{0,2},{1,3},{2,0},{3,1},{4,6},{5,7},{6,4},{7,5},{8,10},{9,11},{10,... | collective-permute-start | bytes 294920 | tf_op jit(solution)/shard_map/ppermute | solution.py:278
  195.2 0.8 copy-start
  196.0 0.6 copy-start.2
  196.7 2.1 collective-permute-start.10
  199.4 18.0 %collective-permute-start.11 = (f32[4,4,2048]{2,0,1:T(4,128)S(1)}, f32[4,4,2048]{2,0,1:T(4,128)S(1)}, u32[]{:S(2)}, u32[]{:S(2)}) collective-permute-start(f32[4,4,2048]{2,0,1:T(4,128)S(1)} %bitcast.79), channel_id=1, source_target_pairs={{0,8},{8,0},{16,24},{24,16},{1,9},{9,1},{17,25},{25,17},{2,10},{10... | collective-permute-start | bytes 393224 | tf_op jit(solution)/shard_map/ppermute | solution.py:278
  200.9 16.4 %collective-permute-start.12 = (f32[4,4,2048]{2,0,1:T(4,128)S(1)}, f32[4,4,2048]{2,0,1:T(4,128)S(1)}, u32[]{:S(2)}, u32[]{:S(2)}) collective-permute-start(f32[4,4,2048]{2,0,1:T(4,128)S(1)} %bitcast.78), channel_id=1, source_target_pairs={{0,16},{8,24},{16,0},{24,8},{1,17},{9,25},{17,1},{25,9},{2,18},{10... | collective-permute-start | bytes 393224 | tf_op jit(solution)/shard_map/ppermute | solution.py:278
  202.4 14.9 %collective-permute-start.13 = (f32[4,4,2048]{2,0,1:T(4,128)S(1)}, f32[4,4,2048]{2,0,1:T(4,128)S(1)}, u32[]{:S(2)}, u32[]{:S(2)}) collective-permute-start(f32[4,4,2048]{2,0,1:T(4,128)S(1)} %bitcast.77), channel_id=1, source_target_pairs={{0,24},{8,16},{16,8},{24,0},{1,25},{9,17},{17,9},{25,1},{2,26},{10... | collective-permute-start | bytes 393224 | tf_op jit(solution)/shard_map/ppermute | solution.py:278
  203.0 23.7 %collective-permute-start.6 = (f32[12,2048]{1,0:T(8,128)S(1)}, f32[12,2048]{1,0:T(8,128)S(1)}, u32[]{:S(2)}, u32[]{:S(2)}) collective-permute-start(f32[12,2048]{1,0:T(8,128)S(1)} %bitcast.75), channel_id=1, source_target_pairs={{0,4},{1,5},{2,6},{3,7},{4,0},{5,1},{6,2},{7,3},{8,12},{9,13},{10,... | collective-permute-start | bytes 294920 | tf_op jit(solution)/shard_map/ppermute | solution.py:278
  215.6 11.1 %collective-permute-start.7 = (f32[12,2048]{1,0:T(8,128)S(1)}, f32[12,2048]{1,0:T(8,128)S(1)}, u32[]{:S(2)}, u32[]{:S(2)}) collective-permute-start(f32[12,2048]{1,0:T(8,128)S(1)} %bitcast.74), channel_id=1, source_target_pairs={{0,6},{1,7},{2,4},{3,5},{4,2},{5,3},{6,0},{7,1},{8,14},{9,15},{10,... | collective-permute-start | bytes 294920 | tf_op jit(solution)/shard_map/ppermute | solution.py:278
  218.1 8.6 %collective-permute-start.16 = (f32[4,2048]{1,0:T(4,128)S(1)}, f32[4,2048]{1,0:T(4,128)S(1)}, u32[]{:S(2)}, u32[]{:S(2)}) collective-permute-start(f32[4,2048]{1,0:T(4,128)S(1)} %get-tuple-element.467), channel_id=1, source_target_pairs={{0,6},{1,7},{2,4},{3,5},{4,2},{5,3},{6,0},{7,1},{8,14},{9,15},{10,... | collective-permute-start | bytes 98312 | tf_op jit(solution)/shard_map/ppermute | solution.py:278
  220.2 9.6 %collective-permute-start.15 = (f32[4,2048]{1,0:T(4,128)S(1)}, f32[4,2048]{1,0:T(4,128)S(1)}, u32[]{:S(2)}, u32[]{:S(2)}) collective-permute-start(f32[4,2048]{1,0:T(4,128)S(1)} %get-tuple-element.468), channel_id=1, source_target_pairs={{0,4},{1,5},{2,6},{3,7},{4,0},{5,1},{6,2},{7,3},{8,12},{9,13},{10,... | collective-permute-start | bytes 98312 | tf_op jit(solution)/shard_map/ppermute | solution.py:278
  223.1 6.7 %collective-permute-start.14 = (f32[4,2048]{1,0:T(4,128)S(1)}, f32[4,2048]{1,0:T(4,128)S(1)}, u32[]{:S(2)}, u32[]{:S(2)}) collective-permute-start(f32[4,2048]{1,0:T(4,128)S(1)} %get-tuple-element.469), channel_id=1, source_target_pairs={{0,2},{1,3},{2,0},{3,1},{4,6},{5,7},{6,4},{7,5},{8,10},{9,11},{10,... | collective-permute-start | bytes 98312 | tf_op jit(solution)/shard_map/ppermute | solution.py:278
  226.7 3.1 %copy-start.3 = (f32[12,2048]{1,0:T(8,128)}, f32[12,2048]{1,0:T(8,128)S(1)}, u32[]{:S(2)}) copy-start(f32[12,2048]{1,0:T(8,128)S(1)} %collective-permute-done.6.refs_2_) | copy-start | bytes 294916
  226.7 3.1 %copy-start.4 = (f32[12,2048]{1,0:T(8,128)}, f32[12,2048]{1,0:T(8,128)S(1)}, u32[]{:S(2)}) copy-start(f32[12,2048]{1,0:T(8,128)S(1)} %collective-permute-done.7.refs_3_) | copy-start | bytes 294916
  226.7 3.1 %copy-start.5 = (f32[4,2048]{1,0:T(4,128)}, f32[4,2048]{1,0:T(4,128)S(1)}, u32[]{:S(2)}) copy-start(f32[4,2048]{1,0:T(4,128)S(1)} %collective-permute-done.16.refs_7_) | copy-start | bytes 98308
  (2 other events, 1.2 us)

commit v5 on v4

--- a/solution.py
+++ b/solution.py
@@ -231,8 +231,8 @@
     )(weights, *after)
 
 
-def held_product_kernel(*refs, block, turned):
-    *left_refs, weight_ref, mine_ref, give_ref = refs
+def held_product_kernel(*refs, count, block, turned):
+    left_refs, weight_ref, (mine_ref, give_ref) = refs[:count], refs[count], refs[-2:]
     piece, columns = mine_ref.shape[1:]
     odd = lax.axis_index("vir") % 2 == 1
 
@@ -257,17 +257,18 @@
             give_ref[unit ^ 1, :, pl.ds(at, block)] = jnp.where(odd, zero, one)
 
 
-def held_product(lefts, weights, block, turned):
+def held_product(lefts, weights, block, turned, after=()):
     shape = (sum(x.shape[0] for x in lefts), lefts[0].shape[2] // 2, weights.shape[1])
     return pl.pallas_call(
-        functools.partial(held_product_kernel, block=block, turned=turned),
-        in_specs=[pl.BlockSpec(memory_space=pltpu.VMEM)] * (1 + len(lefts)),
+        functools.partial(held_product_kernel, count=len(lefts), block=block, turned=turned),
+        in_specs=[pl.BlockSpec(memory_space=pltpu.VMEM)] * (1 + len(lefts))
+        + [pl.BlockSpec(memory_space=pl.ANY)] * len(after),
         out_specs=[pl.BlockSpec(memory_space=pltpu.VMEM)] * 2,
         out_shape=[jax.ShapeDtypeStruct(shape, jnp.float32)] * 2,
         compiler_params=pltpu.CompilerParams(vmem_limit_bytes=HELD),
         cost_estimate=pl.CostEstimate(flops=0, bytes_accessed=0, transcendentals=0),
         name="product_held",
-    )(*lefts, weights)
+    )(*lefts, weights, *after)
 
 
 def pick(x, at, axis):
@@ -322,16 +323,13 @@
 def combined(early, late):
     columns = early[0].shape[1]
     firsts = (early[0].shape[0] + late[0].shape[0]) // 2
-    block = columns // 2
+    vmem = pl.BlockSpec(memory_space=pltpu.VMEM)
     return pl.pallas_call(
         functools.partial(combine_kernel, firsts=firsts),
-        grid_spec=pltpu.PrefetchScalarGridSpec(
-            num_scalar_prefetch=1,
-            grid=(columns // block,),
-            in_specs=[pl.BlockSpec((x.shape[0], block), lambda n, at: (0, n)) for x in (*early, *late)],
-            out_specs=pl.BlockSpec((2 * firsts, block), lambda n, at: (0, n)),
-        ),
+        in_specs=[pl.BlockSpec(memory_space=pltpu.SMEM)] + [vmem] * (len(early) + len(late)),
+        out_specs=vmem,
         out_shape=jax.ShapeDtypeStruct((2 * firsts, columns), jnp.bfloat16),
+        compiler_params=pltpu.CompilerParams(vmem_limit_bytes=8 << 20),
         name="combine",
     )(position(), *early, *late)
 
@@ -365,9 +363,9 @@
     once = 1 + lax.axis_index("vir") // n_vir
     units = n_vir + 2 * len(soon)
     early_sums = lax.fori_loop(0, once, early, jnp.zeros((units, n_z, columns), jnp.float32))
-    mine, give = held_product(last[len(soon) :], held_in_vmem(weights, (early_sums,)), 512, True)
     early_terms = along_z(early_sums, n_vir)
-    [give] = held_back([give], early_terms[:2])
+    held = held_in_vmem(weights, (early_sums,))
+    mine, give = held_product(last[len(soon) :], held, 512, True, after=early_terms[1:2])
     late_sums = over_plane(over_cores(mine, give, n_occ, n_vir), n_occ)
     return combined(early_terms, along_z(late_sums, n_vir))
 

time: 233 us -> 230 us (0.987)
  local copies, waits for them, and re-layouts: 35.9 us -> 33.3 us
    unnamed x21 -> x9, local copies, waits for them, and re-layouts: 26.9 us -> 24.2 us
  transfers between devices with their start and end apart: 18 -> 18, of which waited for: 8 -> 8; matrix products, arithmetic and copies ran while one was open for 16% -> 15% of each run, Pallas kernels for 23% -> 19%
where the time goes in v5:
time: 230 us; the launch traced here: 229 us
  waiting for transfers between devices  95.2 us (41%)
  Pallas kernels  57.7 us (25%)
  starting transfers between devices  38.5 us (17%)
  local copies, waits for them, and re-layouts  33.3 us (14%)
  other arithmetic  3.99 us (2%)
    all_to_all x1, waiting for transfers between devices, on_block(): lax.all_to_all(screened(amplitudes, screen, n_occ, n_vir), 'vir', 0, 0, t...  51.5 us
    ppermute x17, waiting for transfers between devices, exchange(): return lax.ppermute(x, axis_name, [(j, j ^ step) for j in range(size)])  43.8 us
    ppermute x17, starting transfers between devices, exchange(): return lax.ppermute(x, axis_name, [(j, j ^ step) for j in range(size)])  32.2 us
    unnamed x9, local copies, waits for them, and re-layouts  24.2 us
    pallas_call x1, Pallas kernels, product(): pl.pallas_call(functools.partial(product_kernel, count=len(lefts), plain=...  20.2 us
    pallas_call x1, Pallas kernels, held_in_vmem(): pl.pallas_call(hold_kernel, in_specs=[pl.BlockSpec(memory_space=pl.ANY)]...  10.8 us
    pallas_call x1, Pallas kernels, held_product(): pl.pallas_call(functools.partial(held_product_kernel, count=len(lefts), b...  9.56 us
    pallas_call x1, Pallas kernels, given(): pl.pallas_call(functools.partial(give_kernel, steps=steps), grid_spec=plt...  6.45 us
  transfers between devices with their start and end apart: 18, of which 8 were waited for; matrix products, arithmetic and copies ran while one was open for 15% of the time, Pallas kernels for 19%

profile of v5, /device:TPU:0, one launch (start us, length us, event | category | flops | bytes accessed | tf_op | source)
XLA Modules:
  0.0 228.9 jit_solution(6480490135996812049)
XLA Ops:
  0.0 4.2 %screen.1 = bf16[8,16,32,512]{3,2,1,0:T(8,128)(2,1)} custom-call(bf16[4,4,2,2,16,4096]{5,4,3,2,1,0:T(8,128)(2,1)} %bitcast.59, bf16[4,4,2,2,16,4096]{5,4,3,2,1,0:T(8,128)(2,1)} %bitcast.60, bf16[4,4,2,2,16,4096]{5,4,3,2,1,0:T(8,128)(2,1)} %bitcast.61, bf16[4,4,2,2,16,4096]{5,4,3,2,1,0:T(8,128)(2,1)} %bitcast.62, bf16[4,4,2,2,16,4096]{5,4,3,2,1,0:T(8,128)(2,1)} %bitcast.63, ...), custom_call_target="tpu_custom_call" | custom-call | tf_op jit(solution)/shard_map/screen/pallas_call | solution.py:140
  4.2 6.3 %all-to-all-start = ((bf16[8,16,32,512]{3,2,1,0:T(8,128)(2,1)}), bf16[8,16,32,512]{3,2,1,0:T(8,128)(2,1)}, u32[]{:S(2)}, u32[]{:S(2)}) async-start(bf16[8,16,32,512]{3,2,1,0:T(8,128)(2,1)} %screen.1), calls=%async_computation | async-start | bytes 8388608 | tf_op jit(solution)/shard_map/all_to_all | solution.py:349
  10.6 22.7 %copy.8 = bf16[64,32,16,512]{3,1,0,2:T(8,128)(2,1)} copy(bf16[64,32,16,512]{3,2,1,0:T(8,128)(2,1)} %param.6) | data formatting | bytes 67108864 | tf_op args[1]
  33.3 6.4 %give.1 = bf16[4,16,32,512]{3,2,1,0:T(8,128)(2,1)} custom-call(s32[1]{0:T(128)} %bitcast.4.me_ref, bf16[4,4,2,2,16,4096]{5,4,3,2,1,0:T(8,128)(2,1)} %bitcast.67, s32[1,16,64]{2,1,0:T(8,128)} %refs_2_.3, bf16[16,2048,512]{2,1,0:T(8,128)(2,1)} %bitcast.57), custom_call_target="tpu_custom_call" | custom-call | tf_op jit(solution)/shard_map/give/pallas_call | solution.py:61
  40.3 4.0 %collective-permute-done.3.refs_3_.refs_4_ = bf16[4,16,32,512]{3,2,1,0:T(8,128)(2,1)S(1)} collective-permute-done((bf16[4,16,32,512]{3,2,1,0:T(8,128)(2,1)}, bf16[4,16,32,512]{3,2,1,0:T(8,128)(2,1)S(1)}, u32[]{:S(2)}, u32[]{:S(2)}) %collective-permute-start.3) | collective-permute-done | bytes 2097184 | tf_op jit(solution)/shard_map/ppermute | solution.py:279
  45.6 2.8 %keep.2 = (bf16[2,16,32,512]{3,2,1,0:T(8,128)(2,1)}, bf16[2,16,32,512]{3,2,1,0:T(8,128)(2,1)}) custom-call(s32[1]{0:T(128)} %bitcast.4.me_ref, bf16[4,4,2,2,16,4096]{5,4,3,2,1,0:T(8,128)(2,1)} %bitcast.68, bf16[4,4,2,2,16,4096]{5,4,3,2,1,0:T(8,128)(2,1)} %bitcast.69, s32[1,16,64]{2,1,0:T(8,128)} %refs_2_.3, bf16[4,16,32,512]{3,2,1,0:T(8,128)(2,1)} %copy-done, ...), custom_call_target="tpu_custom_call" | custom-call | tf_op jit(solution)/shard_map/keep/pallas_call | solution.py:96
  50.4 2.9 %keep.3 = (bf16[2,16,32,512]{3,2,1,0:T(8,128)(2,1)}, bf16[2,16,32,512]{3,2,1,0:T(8,128)(2,1)}) custom-call(s32[1]{0:T(128)} %bitcast.4.me_ref, bf16[4,4,2,2,16,4096]{5,4,3,2,1,0:T(8,128)(2,1)} %bitcast.70, bf16[4,4,2,2,16,4096]{5,4,3,2,1,0:T(8,128)(2,1)} %bitcast.71, s32[1,16,64]{2,1,0:T(8,128)} %refs_2_.3, bf16[4,16,32,512]{3,2,1,0:T(8,128)(2,1)} %copy-done, ...), custom_call_target="tpu_custom_call" | custom-call | tf_op jit(solution)/shard_map/keep/pallas_call | solution.py:96
  53.2 51.5 %all-to-all-done.refs_2_ = bf16[8,16,32,512]{3,2,1,0:T(8,128)(2,1)} async-done(((bf16[8,16,32,512]{3,2,1,0:T(8,128)(2,1)}), bf16[8,16,32,512]{3,2,1,0:T(8,128)(2,1)}, u32[]{:S(2)}, u32[]{:S(2)}) %all-to-all-start) | async-done | bytes 4194336 | tf_op jit(solution)/shard_map/all_to_all | solution.py:349
  106.9 62.9 %while.14 = (s32[]{:T(128)}, f32[12,4,2048]{2,1,0:T(4,128)}, s32[]{:T(128)}, bf16[8,16,32,512]{3,2,1,0:T(8,128)(2,1)}, bf16[2,16,32,512]{3,2,1,0:T(8,128)(2,1)},...) while((s32[]{:T(128)}, f32[12,4,2048]{2,1,0:T(4,128)}, ...), condition=%wide.region_1.2_spmd, body=%wide.region_0.1_spmd.sunk | while | flops 688134 | bytes 27918648 | solution.py:365
  106.9 20.2 %product.5 = (f32[12,16,2048]{2,1,0:T(8,128)}, f32[12,16,2048]{2,1,0:T(8,128)}) custom-call(s32[1]{0:T(128)} %bitcast.54.me_ref, bf16[8,16,32,512]{3,2,1,0:T(8,128)(2,1)} %get-tuple-element.576.refs_0_, bf16[2,16,32,512]{3,2,1,0:T(8,128)(2,1)} %get-tuple-element.577.refs_1_, bf16[2,16,32,512]{3,2,1,0:T(8,128)(2,1)} %get-tuple-element.578.refs_2_, ...), custom_call_target="tpu_custom_call" | custom-call | tf_op jit(solution)/shard_map/while/body/product/pallas_call | solution.py:193
  127.1 3.6 %collective-permute-done = f32[12,16,2048]{2,1,0:T(8,128)S(1)} collective-permute-done((f32[12,16,2048]{2,1,0:T(8,128)}, f32[12,16,2048]{2,1,0:T(8,128)S(1)}, u32[]{:S(2)}, u32[]{:S(2)}) %collective-permute-start) | collective-permute-done | bytes 1572896 | tf_op jit(solution)/shard_map/while/body/ppermute | solution.py:279
  130.7 2.7 %add.166 = f32[12,16,2048]{2,1,0:T(8,128)} add(f32[12,16,2048]{2,1,0:T(8,128)} %get-tuple-element.541, f32[12,16,2048]{2,1,0:T(8,128)S(1)} %collective-permute-done) | non-fusion elementwise | flops 393216 | bytes 4718592 | tf_op jit(solution)/shard_map/while/body/add | solution.py:283
  133.4 2.7 %reshape.41 = f32[12,2,2,4,2048]{4,3,2,1,0:T(4,128)} reshape(f32[12,16,2048]{2,1,0:T(8,128)} %add.166) | data formatting | bytes 3145728 | tf_op jit(solution)/shard_map/while/body/reshape;while/body/reshape | solution.py:299
  139.3 18.1 %collective-permute-done.1 = f32[12,2,4,2048]{3,2,0,1:T(4,128)S(1)} collective-permute-done((f32[12,2,4,2048]{3,2,0,1:T(4,128)S(1)}, f32[12,2,4,2048]{3,2,0,1:T(4,128)S(1)}, u32[]{:S(2)}, u32[]{:S(2)}) %collective-permute-start.1) | collective-permute-done | bytes 786464 | tf_op jit(solution)/shard_map/while/body/ppermute | solution.py:279
  159.9 9.0 %collective-permute-done.2 = f32[12,1,4,2048]{3,2,0,1:T(4,128)S(1)} collective-permute-done((f32[12,1,4,2048]{3,2,0,1:T(4,128)}, f32[12,1,4,2048]{3,2,0,1:T(4,128)S(1)}, u32[]{:S(2)}, u32[]{:S(2)}) %collective-permute-start.2) | collective-permute-done | bytes 393248 | tf_op jit(solution)/shard_map/while/body/ppermute | solution.py:279
  169.8 2.7 %constant_dynamic-slice_fusion.7 = (f32[12,1,2048]{2,1,0:T(1,128)}, f32[12,1,2048]{2,1,0:T(1,128)S(1)}, f32[12,1,2048]{2,1,0:T(1,128)S(1)}, f32[12,1,2048]{2,1,0:T(1,128)S(1)}) fusion(f32[12,4,2048]{2,1,0:T(4,128)} %get-tuple-element.428.refs_0_, s32[]{:T(128)S(6)} %select_n.100, s32[]{:T(128)S(6)} %select_n.99, s32[]{:T(128)S(6)} %select_n.98, s32[]{:T(128)S(6)} %select_n.97), kind=kLoop, calls=%fused_computation.24 | loop fusion | bytes 786448 | tf_op jit(solution)/shard_map/jit(dynamic_index_in_dim)/dynamic_slice | solution.py:275
  172.5 2.2 collective-permute-start.5
  174.7 10.8 %hold.1.refs_2_ = bf16[16,2048,512]{2,1,0:T(8,128)(2,1)S(1)} custom-call(bf16[16,2048,512]{2,1,0:T(8,128)(2,1)} %get-tuple-element.596, f32[12,4,2048]{2,1,0:T(4,128)} %get-tuple-element.428.refs_0_), custom_call_target="tpu_custom_call" | custom-call | tf_op jit(solution)/shard_map/hold/pallas_call | solution.py:222
  185.5 9.6 %product_held.1 = (f32[4,16,2048]{2,1,0:T(8,128)S(1)}, f32[4,16,2048]{2,1,0:T(8,128)S(1)}) custom-call(bf16[2,16,32,512]{3,2,1,0:T(8,128)(2,1)S(1)} %collective-permute-done.8.refs_0_, bf16[2,16,32,512]{3,2,1,0:T(8,128)(2,1)S(1)} %collective-permute-done.9.refs_1_, bf16[16,2048,512]{2,1,0:T(8,128)(2,1)S(1)} %hold.1.refs_2_, ...), custom_call_target="tpu_custom_call" | custom-call | tf_op jit(solution)/shard_map/product_held/pallas_call | solution.py:262
  201.2 12.7 %collective-permute-start.6 = (f32[12,2048]{1,0:T(8,128)S(1)}, f32[12,2048]{1,0:T(8,128)S(1)}, u32[]{:S(2)}, u32[]{:S(2)}) collective-permute-start(f32[12,2048]{1,0:T(8,128)S(1)} %bitcast.74), channel_id=1, source_target_pairs={{0,4},{1,5},{2,6},{3,7},{4,0},{5,1},{6,2},{7,3},{8,12},{9,13},{10,... | collective-permute-start | bytes 294920 | tf_op jit(solution)/shard_map/ppermute | solution.py:279
  215.9 2.2 collective-permute-start.16
  218.1 2.9 %collective-permute-start.15 = (f32[4,2048]{1,0:T(4,128)S(1)}, f32[4,2048]{1,0:T(4,128)S(1)}, u32[]{:S(2)}, u32[]{:S(2)}) collective-permute-start(f32[4,2048]{1,0:T(4,128)S(1)} %get-tuple-element.468), channel_id=1, source_target_pairs={{0,4},{1,5},{2,6},{3,7},{4,0},{5,1},{6,2},{7,3},{8,12},{9,13},{10,... | collective-permute-start | bytes 98312 | tf_op jit(solution)/shard_map/ppermute | solution.py:279
  221.0 4.4 %collective-permute-done.6.refs_2_ = f32[12,2048]{1,0:T(8,128)S(1)} collective-permute-done((f32[12,2048]{1,0:T(8,128)S(1)}, f32[12,2048]{1,0:T(8,128)S(1)}, u32[]{:S(2)}, u32[]{:S(2)}) %collective-permute-start.6) | collective-permute-done | bytes 98336 | tf_op jit(solution)/shard_map/ppermute | solution.py:279
  225.4 2.8 %collective-permute-done.15.refs_6_ = f32[4,2048]{1,0:T(4,128)S(1)} collective-permute-done((f32[4,2048]{1,0:T(4,128)S(1)}, f32[4,2048]{1,0:T(4,128)S(1)}, u32[]{:S(2)}, u32[]{:S(2)}) %collective-permute-start.15) | collective-permute-done | bytes 32800 | tf_op jit(solution)/shard_map/ppermute | solution.py:279
  (48 shorter events, 21.3 us)
Async XLA Ops:
  4.2 100.5 %all-to-all-start = ((bf16[8,16,32,512]{3,2,1,0:T(8,128)(2,1)}), bf16[8,16,32,512]{3,2,1,0:T(8,128)(2,1)}, u32[]{:S(2)}, u32[]{:S(2)}) async-start(bf16[8,16,32,512]{3,2,1,0:T(8,128)(2,1)} %screen.1), calls=%async_computation | async-start | bytes 8388608 | tf_op jit(solution)/shard_map/all_to_all | solution.py:349
  39.8 4.5 %collective-permute-start.3 = (bf16[4,16,32,512]{3,2,1,0:T(8,128)(2,1)}, bf16[4,16,32,512]{3,2,1,0:T(8,128)(2,1)S(1)}, u32[]{:S(2)}, u32[]{:S(2)}) collective-permute-start(bf16[4,16,32,512]{3,2,1,0:T(8,128)(2,1)} %give.1), channel_id=1, source_target_pairs={{0,1},{1,0},{2,3},{3,2},{4,5},{5,4},{6,7},{7,6},{8,9},{9,8},{10,11... | collective-permute-start | bytes 6291464 | tf_op jit(solution)/shard_map/ppermute | solution.py:279
  44.3 1.4 copy-start
  48.5 57.6 %collective-permute-start.4 = (bf16[2,16,32,512]{3,2,1,0:T(8,128)(2,1)}, bf16[2,16,32,512]{3,2,1,0:T(8,128)(2,1)}, u32[]{:S(2)}, u32[]{:S(2)}) collective-permute-start(bf16[2,16,32,512]{3,2,1,0:T(8,128)(2,1)} %get-tuple-element.427), channel_id=1, source_target_pairs={{0,2},{1,3},{2,0},{3,1},{4,6},{5,7},{6,4},{7,5},{8,10},{9,11},{10,... | collective-permute-start | bytes 3145736 | tf_op jit(solution)/shard_map/ppermute | solution.py:279
  104.7 80.8 %collective-permute-start.8 = (bf16[2,16,32,512]{3,2,1,0:T(8,128)(2,1)}, bf16[2,16,32,512]{3,2,1,0:T(8,128)(2,1)S(1)}, u32[]{:S(2)}, u32[]{:S(2)}) collective-permute-start(bf16[2,16,32,512]{3,2,1,0:T(8,128)(2,1)} %get-tuple-element.431), channel_id=1, source_target_pairs={{0,4},{1,5},{2,6},{3,7},{4,0},{5,1},{6,2},{7,3},{8,12},{9,13},{10,... | collective-permute-start | bytes 3145736 | tf_op jit(solution)/shard_map/ppermute | solution.py:279
  104.7 80.8 %collective-permute-start.9 = (bf16[2,16,32,512]{3,2,1,0:T(8,128)(2,1)}, bf16[2,16,32,512]{3,2,1,0:T(8,128)(2,1)S(1)}, u32[]{:S(2)}, u32[]{:S(2)}) collective-permute-start(bf16[2,16,32,512]{3,2,1,0:T(8,128)(2,1)} %get-tuple-element.432), channel_id=1, source_target_pairs={{0,6},{1,7},{2,4},{3,5},{4,2},{5,3},{6,0},{7,1},{8,14},{9,15},{10,... | collective-permute-start | bytes 3145736 | tf_op jit(solution)/shard_map/ppermute | solution.py:279
  127.1 3.6 %collective-permute-start = (f32[12,16,2048]{2,1,0:T(8,128)}, f32[12,16,2048]{2,1,0:T(8,128)S(1)}, u32[]{:S(2)}, u32[]{:S(2)}) collective-permute-start(f32[12,16,2048]{2,1,0:T(8,128)} %get-tuple-element.542), channel_id=1, source_target_pairs={{0,1},{1,0},{2,3},{3,2},{4,5},{5,4},{6,7},{7,6},{8,9},{9,8},{10,11... | collective-permute-start | bytes 4718600 | tf_op jit(solution)/shard_map/while/body/ppermute | solution.py:279
  137.8 19.6 %collective-permute-start.1 = (f32[12,2,4,2048]{3,2,0,1:T(4,128)S(1)}, f32[12,2,4,2048]{3,2,0,1:T(4,128)S(1)}, u32[]{:S(2)}, u32[]{:S(2)}) collective-permute-start(f32[12,2,4,2048]{3,2,0,1:T(4,128)S(1)} %bitcast.72), channel_id=1, source_target_pairs={{0,8},{8,0},{16,24},{24,16},{1,9},{9,1},{17,25},{25,17},{2,10},{10... | collective-permute-start | bytes 2359304 | tf_op jit(solution)/shard_map/while/body/ppermute | solution.py:279
  158.4 10.5 %collective-permute-start.2 = (f32[12,1,4,2048]{3,2,0,1:T(4,128)}, f32[12,1,4,2048]{3,2,0,1:T(4,128)S(1)}, u32[]{:S(2)}, u32[]{:S(2)}) collective-permute-start(f32[12,1,4,2048]{3,2,0,1:T(4,128)} %constant_dynamic-slice_fusion.14), channel_id=1, source_target_pairs={{0,16},{8,24},{16,0},{24,8},{1,17},{9,25},{17,1},{25,9},{2,18},{10... | collective-permute-start | bytes 1179656 | tf_op jit(solution)/shard_map/while/body/ppermute | solution.py:279
  172.5 13.0 %collective-permute-start.5 = (f32[12,2048]{1,0:T(8,128)S(1)}, f32[12,2048]{1,0:T(8,128)S(1)}, u32[]{:S(2)}, u32[]{:S(2)}) collective-permute-start(f32[12,2048]{1,0:T(8,128)S(1)} %bitcast.75), channel_id=1, source_target_pairs={{0,2},{1,3},{2,0},{3,1},{4,6},{5,7},{6,4},{7,5},{8,10},{9,11},{10,... | collective-permute-start | bytes 294920 | tf_op jit(solution)/shard_map/ppermute | solution.py:279
  195.1 2.0 collective-permute-start.10
  197.0 4.1 %copy-start.1 = (f32[12,1,2048]{2,1,0:T(1,128)S(1)}, f32[12,1,2048]{2,1,0:T(1,128)}, u32[]{:S(2)}) copy-start(f32[12,1,2048]{2,1,0:T(1,128)} %get-tuple-element.463) | copy-start | bytes 294916
  197.6 18.1 %collective-permute-start.11 = (f32[4,4,2048]{2,0,1:T(4,128)S(1)}, f32[4,4,2048]{2,0,1:T(4,128)S(1)}, u32[]{:S(2)}, u32[]{:S(2)}) collective-permute-start(f32[4,4,2048]{2,0,1:T(4,128)S(1)} %bitcast.78), channel_id=1, source_target_pairs={{0,8},{8,0},{16,24},{24,16},{1,9},{9,1},{17,25},{25,17},{2,10},{10... | collective-permute-start | bytes 393224 | tf_op jit(solution)/shard_map/ppermute | solution.py:279
  199.2 16.6 %collective-permute-start.12 = (f32[4,4,2048]{2,0,1:T(4,128)S(1)}, f32[4,4,2048]{2,0,1:T(4,128)S(1)}, u32[]{:S(2)}, u32[]{:S(2)}) collective-permute-start(f32[4,4,2048]{2,0,1:T(4,128)S(1)} %bitcast.77), channel_id=1, source_target_pairs={{0,16},{8,24},{16,0},{24,8},{1,17},{9,25},{17,1},{25,9},{2,18},{10... | collective-permute-start | bytes 393224 | tf_op jit(solution)/shard_map/ppermute | solution.py:279
  200.7 15.1 %collective-permute-start.13 = (f32[4,4,2048]{2,0,1:T(4,128)S(1)}, f32[4,4,2048]{2,0,1:T(4,128)S(1)}, u32[]{:S(2)}, u32[]{:S(2)}) collective-permute-start(f32[4,4,2048]{2,0,1:T(4,128)S(1)} %bitcast.76), channel_id=1, source_target_pairs={{0,24},{8,16},{16,8},{24,0},{1,25},{9,17},{17,9},{25,1},{2,26},{10... | collective-permute-start | bytes 393224 | tf_op jit(solution)/shard_map/ppermute | solution.py:279
  201.2 24.2 %collective-permute-start.6 = (f32[12,2048]{1,0:T(8,128)S(1)}, f32[12,2048]{1,0:T(8,128)S(1)}, u32[]{:S(2)}, u32[]{:S(2)}) collective-permute-start(f32[12,2048]{1,0:T(8,128)S(1)} %bitcast.74), channel_id=1, source_target_pairs={{0,4},{1,5},{2,6},{3,7},{4,0},{5,1},{6,2},{7,3},{8,12},{9,13},{10,... | collective-permute-start | bytes 294920 | tf_op jit(solution)/shard_map/ppermute | solution.py:279
  214.0 11.4 %collective-permute-start.7 = (f32[12,2048]{1,0:T(8,128)S(1)}, f32[12,2048]{1,0:T(8,128)S(1)}, u32[]{:S(2)}, u32[]{:S(2)}) collective-permute-start(f32[12,2048]{1,0:T(8,128)S(1)} %bitcast.73), channel_id=1, source_target_pairs={{0,6},{1,7},{2,4},{3,5},{4,2},{5,3},{6,0},{7,1},{8,14},{9,15},{10,... | collective-permute-start | bytes 294920 | tf_op jit(solution)/shard_map/ppermute | solution.py:279
  215.9 9.5 %collective-permute-start.16 = (f32[4,2048]{1,0:T(4,128)S(1)}, f32[4,2048]{1,0:T(4,128)S(1)}, u32[]{:S(2)}, u32[]{:S(2)}) collective-permute-start(f32[4,2048]{1,0:T(4,128)S(1)} %get-tuple-element.467), channel_id=1, source_target_pairs={{0,6},{1,7},{2,4},{3,5},{4,2},{5,3},{6,0},{7,1},{8,14},{9,15},{10,... | collective-permute-start | bytes 98312 | tf_op jit(solution)/shard_map/ppermute | solution.py:279
  218.1 10.1 %collective-permute-start.15 = (f32[4,2048]{1,0:T(4,128)S(1)}, f32[4,2048]{1,0:T(4,128)S(1)}, u32[]{:S(2)}, u32[]{:S(2)}) collective-permute-start(f32[4,2048]{1,0:T(4,128)S(1)} %get-tuple-element.468), channel_id=1, source_target_pairs={{0,4},{1,5},{2,6},{3,7},{4,0},{5,1},{6,2},{7,3},{8,12},{9,13},{10,... | collective-permute-start | bytes 98312 | tf_op jit(solution)/shard_map/ppermute | solution.py:279
  221.0 7.2 %collective-permute-start.14 = (f32[4,2048]{1,0:T(4,128)S(1)}, f32[4,2048]{1,0:T(4,128)S(1)}, u32[]{:S(2)}, u32[]{:S(2)}) collective-permute-start(f32[4,2048]{1,0:T(4,128)S(1)} %get-tuple-element.469), channel_id=1, source_target_pairs={{0,2},{1,3},{2,0},{3,1},{4,6},{5,7},{6,4},{7,5},{8,10},{9,11},{10,... | collective-permute-start | bytes 98312 | tf_op jit(solution)/shard_map/ppermute | solution.py:279

commit v6 on v5

--- a/solution.py
+++ b/solution.py
@@ -365,7 +365,7 @@
     early_sums = lax.fori_loop(0, once, early, jnp.zeros((units, n_z, columns), jnp.float32))
     early_terms = along_z(early_sums, n_vir)
     held = held_in_vmem(weights, (early_sums,))
-    mine, give = held_product(last[len(soon) :], held, 512, True, after=early_terms[1:2])
+    mine, give = held_product(last[len(soon) :], held, 1024, True, after=early_terms[1:2])
     late_sums = over_plane(over_cores(mine, give, n_occ, n_vir), n_occ)
     return combined(early_terms, along_z(late_sums, n_vir))
 

time: 230 us -> 229 us (level)
  transfers between devices with their start and end apart: 18 -> 18, of which waited for: 8 -> 8; matrix products, arithmetic and copies ran while one was open for 15% -> 16% of each run, Pallas kernels for 19% -> 19%
where the time goes in v6:
time: 229 us; the launch traced here: 228 us
  waiting for transfers between devices  95.2 us (42%)
  Pallas kernels  57.2 us (25%)
  starting transfers between devices  38.5 us (17%)
  local copies, waits for them, and re-layouts  33.3 us (15%)
  other arithmetic  3.99 us (2%)
    all_to_all x1, waiting for transfers between devices, on_block(): lax.all_to_all(screened(amplitudes, screen, n_occ, n_vir), 'vir', 0, 0, t...  51.5 us
    ppermute x17, waiting for transfers between devices, exchange(): return lax.ppermute(x, axis_name, [(j, j ^ step) for j in range(size)])  43.8 us
    ppermute x17, starting transfers between devices, exchange(): return lax.ppermute(x, axis_name, [(j, j ^ step) for j in range(size)])  32.2 us
    unnamed x9, local copies, waits for them, and re-layouts  24.2 us
    pallas_call x1, Pallas kernels, product(): pl.pallas_call(functools.partial(product_kernel, count=len(lefts), plain=...  20.2 us
    pallas_call x1, Pallas kernels, held_in_vmem(): pl.pallas_call(hold_kernel, in_specs=[pl.BlockSpec(memory_space=pl.ANY)]...  10.8 us
    pallas_call x1, Pallas kernels, held_product(): pl.pallas_call(functools.partial(held_product_kernel, count=len(lefts), b...  9.09 us
    pallas_call x1, Pallas kernels, given(): pl.pallas_call(functools.partial(give_kernel, steps=steps), grid_spec=plt...  6.45 us
  transfers between devices with their start and end apart: 18, of which 8 were waited for; matrix products, arithmetic and copies ran while one was open for 16% of the time, Pallas kernels for 19%

profile of v6, /device:TPU:0, one launch (start us, length us, event | category | flops | bytes accessed | tf_op | source)
XLA Modules:
  0.0 228.5 jit_solution(16439883495284329150)
XLA Ops:
  0.0 4.2 %screen.1 = bf16[8,16,32,512]{3,2,1,0:T(8,128)(2,1)} custom-call(bf16[4,4,2,2,16,4096]{5,4,3,2,1,0:T(8,128)(2,1)} %bitcast.59, bf16[4,4,2,2,16,4096]{5,4,3,2,1,0:T(8,128)(2,1)} %bitcast.60, bf16[4,4,2,2,16,4096]{5,4,3,2,1,0:T(8,128)(2,1)} %bitcast.61, bf16[4,4,2,2,16,4096]{5,4,3,2,1,0:T(8,128)(2,1)} %bitcast.62, bf16[4,4,2,2,16,4096]{5,4,3,2,1,0:T(8,128)(2,1)} %bitcast.63, ...), custom_call_target="tpu_custom_call" | custom-call | tf_op jit(solution)/shard_map/screen/pallas_call | solution.py:140
  4.2 6.3 %all-to-all-start = ((bf16[8,16,32,512]{3,2,1,0:T(8,128)(2,1)}), bf16[8,16,32,512]{3,2,1,0:T(8,128)(2,1)}, u32[]{:S(2)}, u32[]{:S(2)}) async-start(bf16[8,16,32,512]{3,2,1,0:T(8,128)(2,1)} %screen.1), calls=%async_computation | async-start | bytes 8388608 | tf_op jit(solution)/shard_map/all_to_all | solution.py:349
  10.6 22.7 %copy.8 = bf16[64,32,16,512]{3,1,0,2:T(8,128)(2,1)} copy(bf16[64,32,16,512]{3,2,1,0:T(8,128)(2,1)} %param.6) | data formatting | bytes 67108864 | tf_op args[1]
  33.3 6.4 %give.1 = bf16[4,16,32,512]{3,2,1,0:T(8,128)(2,1)} custom-call(s32[1]{0:T(128)} %bitcast.4.me_ref, bf16[4,4,2,2,16,4096]{5,4,3,2,1,0:T(8,128)(2,1)} %bitcast.67, s32[1,16,64]{2,1,0:T(8,128)} %refs_2_.3, bf16[16,2048,512]{2,1,0:T(8,128)(2,1)} %bitcast.57), custom_call_target="tpu_custom_call" | custom-call | tf_op jit(solution)/shard_map/give/pallas_call | solution.py:61
  40.3 4.0 %collective-permute-done.3.refs_3_.refs_4_ = bf16[4,16,32,512]{3,2,1,0:T(8,128)(2,1)S(1)} collective-permute-done((bf16[4,16,32,512]{3,2,1,0:T(8,128)(2,1)}, bf16[4,16,32,512]{3,2,1,0:T(8,128)(2,1)S(1)}, u32[]{:S(2)}, u32[]{:S(2)}) %collective-permute-start.3) | collective-permute-done | bytes 2097184 | tf_op jit(solution)/shard_map/ppermute | solution.py:279
  45.6 2.8 %keep.2 = (bf16[2,16,32,512]{3,2,1,0:T(8,128)(2,1)}, bf16[2,16,32,512]{3,2,1,0:T(8,128)(2,1)}) custom-call(s32[1]{0:T(128)} %bitcast.4.me_ref, bf16[4,4,2,2,16,4096]{5,4,3,2,1,0:T(8,128)(2,1)} %bitcast.68, bf16[4,4,2,2,16,4096]{5,4,3,2,1,0:T(8,128)(2,1)} %bitcast.69, s32[1,16,64]{2,1,0:T(8,128)} %refs_2_.3, bf16[4,16,32,512]{3,2,1,0:T(8,128)(2,1)} %copy-done, ...), custom_call_target="tpu_custom_call" | custom-call | tf_op jit(solution)/shard_map/keep/pallas_call | solution.py:96
  50.4 2.9 %keep.3 = (bf16[2,16,32,512]{3,2,1,0:T(8,128)(2,1)}, bf16[2,16,32,512]{3,2,1,0:T(8,128)(2,1)}) custom-call(s32[1]{0:T(128)} %bitcast.4.me_ref, bf16[4,4,2,2,16,4096]{5,4,3,2,1,0:T(8,128)(2,1)} %bitcast.70, bf16[4,4,2,2,16,4096]{5,4,3,2,1,0:T(8,128)(2,1)} %bitcast.71, s32[1,16,64]{2,1,0:T(8,128)} %refs_2_.3, bf16[4,16,32,512]{3,2,1,0:T(8,128)(2,1)} %copy-done, ...), custom_call_target="tpu_custom_call" | custom-call | tf_op jit(solution)/shard_map/keep/pallas_call | solution.py:96
  53.2 51.5 %all-to-all-done.refs_2_ = bf16[8,16,32,512]{3,2,1,0:T(8,128)(2,1)} async-done(((bf16[8,16,32,512]{3,2,1,0:T(8,128)(2,1)}), bf16[8,16,32,512]{3,2,1,0:T(8,128)(2,1)}, u32[]{:S(2)}, u32[]{:S(2)}) %all-to-all-start) | async-done | bytes 4194336 | tf_op jit(solution)/shard_map/all_to_all | solution.py:349
  106.9 62.9 %while.14 = (s32[]{:T(128)}, f32[12,4,2048]{2,1,0:T(4,128)}, s32[]{:T(128)}, bf16[8,16,32,512]{3,2,1,0:T(8,128)(2,1)}, bf16[2,16,32,512]{3,2,1,0:T(8,128)(2,1)},...) while((s32[]{:T(128)}, f32[12,4,2048]{2,1,0:T(4,128)}, ...), condition=%wide.region_1.2_spmd, body=%wide.region_0.1_spmd.sunk | while | flops 688134 | bytes 27918648 | solution.py:365
  106.9 20.2 %product.5 = (f32[12,16,2048]{2,1,0:T(8,128)}, f32[12,16,2048]{2,1,0:T(8,128)}) custom-call(s32[1]{0:T(128)} %bitcast.54.me_ref, bf16[8,16,32,512]{3,2,1,0:T(8,128)(2,1)} %get-tuple-element.576.refs_0_, bf16[2,16,32,512]{3,2,1,0:T(8,128)(2,1)} %get-tuple-element.577.refs_1_, bf16[2,16,32,512]{3,2,1,0:T(8,128)(2,1)} %get-tuple-element.578.refs_2_, ...), custom_call_target="tpu_custom_call" | custom-call | tf_op jit(solution)/shard_map/while/body/product/pallas_call | solution.py:193
  127.1 3.6 %collective-permute-done = f32[12,16,2048]{2,1,0:T(8,128)S(1)} collective-permute-done((f32[12,16,2048]{2,1,0:T(8,128)}, f32[12,16,2048]{2,1,0:T(8,128)S(1)}, u32[]{:S(2)}, u32[]{:S(2)}) %collective-permute-start) | collective-permute-done | bytes 1572896 | tf_op jit(solution)/shard_map/while/body/ppermute | solution.py:279
  130.7 2.7 %add.166 = f32[12,16,2048]{2,1,0:T(8,128)} add(f32[12,16,2048]{2,1,0:T(8,128)} %get-tuple-element.541, f32[12,16,2048]{2,1,0:T(8,128)S(1)} %collective-permute-done) | non-fusion elementwise | flops 393216 | bytes 4718592 | tf_op jit(solution)/shard_map/while/body/add | solution.py:283
  133.4 2.7 %reshape.41 = f32[12,2,2,4,2048]{4,3,2,1,0:T(4,128)} reshape(f32[12,16,2048]{2,1,0:T(8,128)} %add.166) | data formatting | bytes 3145728 | tf_op jit(solution)/shard_map/while/body/reshape;while/body/reshape | solution.py:299
  139.3 18.1 %collective-permute-done.1 = f32[12,2,4,2048]{3,2,0,1:T(4,128)S(1)} collective-permute-done((f32[12,2,4,2048]{3,2,0,1:T(4,128)S(1)}, f32[12,2,4,2048]{3,2,0,1:T(4,128)S(1)}, u32[]{:S(2)}, u32[]{:S(2)}) %collective-permute-start.1) | collective-permute-done | bytes 786464 | tf_op jit(solution)/shard_map/while/body/ppermute | solution.py:279
  159.9 9.0 %collective-permute-done.2 = f32[12,1,4,2048]{3,2,0,1:T(4,128)S(1)} collective-permute-done((f32[12,1,4,2048]{3,2,0,1:T(4,128)}, f32[12,1,4,2048]{3,2,0,1:T(4,128)S(1)}, u32[]{:S(2)}, u32[]{:S(2)}) %collective-permute-start.2) | collective-permute-done | bytes 393248 | tf_op jit(solution)/shard_map/while/body/ppermute | solution.py:279
  169.8 2.7 %constant_dynamic-slice_fusion.7 = (f32[12,1,2048]{2,1,0:T(1,128)}, f32[12,1,2048]{2,1,0:T(1,128)S(1)}, f32[12,1,2048]{2,1,0:T(1,128)S(1)}, f32[12,1,2048]{2,1,0:T(1,128)S(1)}) fusion(f32[12,4,2048]{2,1,0:T(4,128)} %get-tuple-element.428.refs_0_, s32[]{:T(128)S(6)} %select_n.100, s32[]{:T(128)S(6)} %select_n.99, s32[]{:T(128)S(6)} %select_n.98, s32[]{:T(128)S(6)} %select_n.97), kind=kLoop, calls=%fused_computation.24 | loop fusion | bytes 786448 | tf_op jit(solution)/shard_map/jit(dynamic_index_in_dim)/dynamic_slice | solution.py:275
  172.5 2.2 collective-permute-start.5
  174.7 10.8 %hold.1.refs_2_ = bf16[16,2048,512]{2,1,0:T(8,128)(2,1)S(1)} custom-call(bf16[16,2048,512]{2,1,0:T(8,128)(2,1)} %get-tuple-element.596, f32[12,4,2048]{2,1,0:T(4,128)} %get-tuple-element.428.refs_0_), custom_call_target="tpu_custom_call" | custom-call | tf_op jit(solution)/shard_map/hold/pallas_call | solution.py:222
  185.5 9.1 %product_held.1 = (f32[4,16,2048]{2,1,0:T(8,128)S(1)}, f32[4,16,2048]{2,1,0:T(8,128)S(1)}) custom-call(bf16[2,16,32,512]{3,2,1,0:T(8,128)(2,1)S(1)} %collective-permute-done.8.refs_0_, bf16[2,16,32,512]{3,2,1,0:T(8,128)(2,1)S(1)} %collective-permute-done.9.refs_1_, bf16[16,2048,512]{2,1,0:T(8,128)(2,1)S(1)} %hold.1.refs_2_, ...), custom_call_target="tpu_custom_call" | custom-call | tf_op jit(solution)/shard_map/product_held/pallas_call | solution.py:262
  200.8 12.7 %collective-permute-start.6 = (f32[12,2048]{1,0:T(8,128)S(1)}, f32[12,2048]{1,0:T(8,128)S(1)}, u32[]{:S(2)}, u32[]{:S(2)}) collective-permute-start(f32[12,2048]{1,0:T(8,128)S(1)} %bitcast.74), channel_id=1, source_target_pairs={{0,4},{1,5},{2,6},{3,7},{4,0},{5,1},{6,2},{7,3},{8,12},{9,13},{10,... | collective-permute-start | bytes 294920 | tf_op jit(solution)/shard_map/ppermute | solution.py:279
  215.4 2.2 collective-permute-start.16
  217.6 2.9 %collective-permute-start.15 = (f32[4,2048]{1,0:T(4,128)S(1)}, f32[4,2048]{1,0:T(4,128)S(1)}, u32[]{:S(2)}, u32[]{:S(2)}) collective-permute-start(f32[4,2048]{1,0:T(4,128)S(1)} %get-tuple-element.468), channel_id=1, source_target_pairs={{0,4},{1,5},{2,6},{3,7},{4,0},{5,1},{6,2},{7,3},{8,12},{9,13},{10,... | collective-permute-start | bytes 98312 | tf_op jit(solution)/shard_map/ppermute | solution.py:279
  220.6 4.4 %collective-permute-done.6.refs_2_ = f32[12,2048]{1,0:T(8,128)S(1)} collective-permute-done((f32[12,2048]{1,0:T(8,128)S(1)}, f32[12,2048]{1,0:T(8,128)S(1)}, u32[]{:S(2)}, u32[]{:S(2)}) %collective-permute-start.6) | collective-permute-done | bytes 98336 | tf_op jit(solution)/shard_map/ppermute | solution.py:279
  225.0 2.8 %collective-permute-done.15.refs_6_ = f32[4,2048]{1,0:T(4,128)S(1)} collective-permute-done((f32[4,2048]{1,0:T(4,128)S(1)}, f32[4,2048]{1,0:T(4,128)S(1)}, u32[]{:S(2)}, u32[]{:S(2)}) %collective-permute-start.15) | collective-permute-done | bytes 32800 | tf_op jit(solution)/shard_map/ppermute | solution.py:279
  (48 shorter events, 21.3 us)
Async XLA Ops:
  4.2 100.5 %all-to-all-start = ((bf16[8,16,32,512]{3,2,1,0:T(8,128)(2,1)}), bf16[8,16,32,512]{3,2,1,0:T(8,128)(2,1)}, u32[]{:S(2)}, u32[]{:S(2)}) async-start(bf16[8,16,32,512]{3,2,1,0:T(8,128)(2,1)} %screen.1), calls=%async_computation | async-start | bytes 8388608 | tf_op jit(solution)/shard_map/all_to_all | solution.py:349
  39.8 4.5 %collective-permute-start.3 = (bf16[4,16,32,512]{3,2,1,0:T(8,128)(2,1)}, bf16[4,16,32,512]{3,2,1,0:T(8,128)(2,1)S(1)}, u32[]{:S(2)}, u32[]{:S(2)}) collective-permute-start(bf16[4,16,32,512]{3,2,1,0:T(8,128)(2,1)} %give.1), channel_id=1, source_target_pairs={{0,1},{1,0},{2,3},{3,2},{4,5},{5,4},{6,7},{7,6},{8,9},{9,8},{10,11... | collective-permute-start | bytes 6291464 | tf_op jit(solution)/shard_map/ppermute | solution.py:279
  44.3 1.4 copy-start
  48.5 57.6 %collective-permute-start.4 = (bf16[2,16,32,512]{3,2,1,0:T(8,128)(2,1)}, bf16[2,16,32,512]{3,2,1,0:T(8,128)(2,1)}, u32[]{:S(2)}, u32[]{:S(2)}) collective-permute-start(bf16[2,16,32,512]{3,2,1,0:T(8,128)(2,1)} %get-tuple-element.427), channel_id=1, source_target_pairs={{0,2},{1,3},{2,0},{3,1},{4,6},{5,7},{6,4},{7,5},{8,10},{9,11},{10,... | collective-permute-start | bytes 3145736 | tf_op jit(solution)/shard_map/ppermute | solution.py:279
  104.7 80.8 %collective-permute-start.8 = (bf16[2,16,32,512]{3,2,1,0:T(8,128)(2,1)}, bf16[2,16,32,512]{3,2,1,0:T(8,128)(2,1)S(1)}, u32[]{:S(2)}, u32[]{:S(2)}) collective-permute-start(bf16[2,16,32,512]{3,2,1,0:T(8,128)(2,1)} %get-tuple-element.431), channel_id=1, source_target_pairs={{0,4},{1,5},{2,6},{3,7},{4,0},{5,1},{6,2},{7,3},{8,12},{9,13},{10,... | collective-permute-start | bytes 3145736 | tf_op jit(solution)/shard_map/ppermute | solution.py:279
  104.7 80.8 %collective-permute-start.9 = (bf16[2,16,32,512]{3,2,1,0:T(8,128)(2,1)}, bf16[2,16,32,512]{3,2,1,0:T(8,128)(2,1)S(1)}, u32[]{:S(2)}, u32[]{:S(2)}) collective-permute-start(bf16[2,16,32,512]{3,2,1,0:T(8,128)(2,1)} %get-tuple-element.432), channel_id=1, source_target_pairs={{0,6},{1,7},{2,4},{3,5},{4,2},{5,3},{6,0},{7,1},{8,14},{9,15},{10,... | collective-permute-start | bytes 3145736 | tf_op jit(solution)/shard_map/ppermute | solution.py:279
  127.1 3.6 %collective-permute-start = (f32[12,16,2048]{2,1,0:T(8,128)}, f32[12,16,2048]{2,1,0:T(8,128)S(1)}, u32[]{:S(2)}, u32[]{:S(2)}) collective-permute-start(f32[12,16,2048]{2,1,0:T(8,128)} %get-tuple-element.542), channel_id=1, source_target_pairs={{0,1},{1,0},{2,3},{3,2},{4,5},{5,4},{6,7},{7,6},{8,9},{9,8},{10,11... | collective-permute-start | bytes 4718600 | tf_op jit(solution)/shard_map/while/body/ppermute | solution.py:279
  137.8 19.6 %collective-permute-start.1 = (f32[12,2,4,2048]{3,2,0,1:T(4,128)S(1)}, f32[12,2,4,2048]{3,2,0,1:T(4,128)S(1)}, u32[]{:S(2)}, u32[]{:S(2)}) collective-permute-start(f32[12,2,4,2048]{3,2,0,1:T(4,128)S(1)} %bitcast.72), channel_id=1, source_target_pairs={{0,8},{8,0},{16,24},{24,16},{1,9},{9,1},{17,25},{25,17},{2,10},{10... | collective-permute-start | bytes 2359304 | tf_op jit(solution)/shard_map/while/body/ppermute | solution.py:279
  158.4 10.5 %collective-permute-start.2 = (f32[12,1,4,2048]{3,2,0,1:T(4,128)}, f32[12,1,4,2048]{3,2,0,1:T(4,128)S(1)}, u32[]{:S(2)}, u32[]{:S(2)}) collective-permute-start(f32[12,1,4,2048]{3,2,0,1:T(4,128)} %constant_dynamic-slice_fusion.14), channel_id=1, source_target_pairs={{0,16},{8,24},{16,0},{24,8},{1,17},{9,25},{17,1},{25,9},{2,18},{10... | collective-permute-start | bytes 1179656 | tf_op jit(solution)/shard_map/while/body/ppermute | solution.py:279
  172.5 13.0 %collective-permute-start.5 = (f32[12,2048]{1,0:T(8,128)S(1)}, f32[12,2048]{1,0:T(8,128)S(1)}, u32[]{:S(2)}, u32[]{:S(2)}) collective-permute-start(f32[12,2048]{1,0:T(8,128)S(1)} %bitcast.75), channel_id=1, source_target_pairs={{0,2},{1,3},{2,0},{3,1},{4,6},{5,7},{6,4},{7,5},{8,10},{9,11},{10,... | collective-permute-start | bytes 294920 | tf_op jit(solution)/shard_map/ppermute | solution.py:279
  194.6 2.0 collective-permute-start.10
  196.6 4.1 %copy-start.1 = (f32[12,1,2048]{2,1,0:T(1,128)S(1)}, f32[12,1,2048]{2,1,0:T(1,128)}, u32[]{:S(2)}) copy-start(f32[12,1,2048]{2,1,0:T(1,128)} %get-tuple-element.463) | copy-start | bytes 294916
  197.1 18.1 %collective-permute-start.11 = (f32[4,4,2048]{2,0,1:T(4,128)S(1)}, f32[4,4,2048]{2,0,1:T(4,128)S(1)}, u32[]{:S(2)}, u32[]{:S(2)}) collective-permute-start(f32[4,4,2048]{2,0,1:T(4,128)S(1)} %bitcast.78), channel_id=1, source_target_pairs={{0,8},{8,0},{16,24},{24,16},{1,9},{9,1},{17,25},{25,17},{2,10},{10... | collective-permute-start | bytes 393224 | tf_op jit(solution)/shard_map/ppermute | solution.py:279
  198.7 16.6 %collective-permute-start.12 = (f32[4,4,2048]{2,0,1:T(4,128)S(1)}, f32[4,4,2048]{2,0,1:T(4,128)S(1)}, u32[]{:S(2)}, u32[]{:S(2)}) collective-permute-start(f32[4,4,2048]{2,0,1:T(4,128)S(1)} %bitcast.77), channel_id=1, source_target_pairs={{0,16},{8,24},{16,0},{24,8},{1,17},{9,25},{17,1},{25,9},{2,18},{10... | collective-permute-start | bytes 393224 | tf_op jit(solution)/shard_map/ppermute | solution.py:279
  200.2 15.1 %collective-permute-start.13 = (f32[4,4,2048]{2,0,1:T(4,128)S(1)}, f32[4,4,2048]{2,0,1:T(4,128)S(1)}, u32[]{:S(2)}, u32[]{:S(2)}) collective-permute-start(f32[4,4,2048]{2,0,1:T(4,128)S(1)} %bitcast.76), channel_id=1, source_target_pairs={{0,24},{8,16},{16,8},{24,0},{1,25},{9,17},{17,9},{25,1},{2,26},{10... | collective-permute-start | bytes 393224 | tf_op jit(solution)/shard_map/ppermute | solution.py:279
  200.8 24.2 %collective-permute-start.6 = (f32[12,2048]{1,0:T(8,128)S(1)}, f32[12,2048]{1,0:T(8,128)S(1)}, u32[]{:S(2)}, u32[]{:S(2)}) collective-permute-start(f32[12,2048]{1,0:T(8,128)S(1)} %bitcast.74), channel_id=1, source_target_pairs={{0,4},{1,5},{2,6},{3,7},{4,0},{5,1},{6,2},{7,3},{8,12},{9,13},{10,... | collective-permute-start | bytes 294920 | tf_op jit(solution)/shard_map/ppermute | solution.py:279
  213.5 11.4 %collective-permute-start.7 = (f32[12,2048]{1,0:T(8,128)S(1)}, f32[12,2048]{1,0:T(8,128)S(1)}, u32[]{:S(2)}, u32[]{:S(2)}) collective-permute-start(f32[12,2048]{1,0:T(8,128)S(1)} %bitcast.73), channel_id=1, source_target_pairs={{0,6},{1,7},{2,4},{3,5},{4,2},{5,3},{6,0},{7,1},{8,14},{9,15},{10,... | collective-permute-start | bytes 294920 | tf_op jit(solution)/shard_map/ppermute | solution.py:279
  215.4 9.5 %collective-permute-start.16 = (f32[4,2048]{1,0:T(4,128)S(1)}, f32[4,2048]{1,0:T(4,128)S(1)}, u32[]{:S(2)}, u32[]{:S(2)}) collective-permute-start(f32[4,2048]{1,0:T(4,128)S(1)} %get-tuple-element.467), channel_id=1, source_target_pairs={{0,6},{1,7},{2,4},{3,5},{4,2},{5,3},{6,0},{7,1},{8,14},{9,15},{10,... | collective-permute-start | bytes 98312 | tf_op jit(solution)/shard_map/ppermute | solution.py:279
  217.6 10.1 %collective-permute-start.15 = (f32[4,2048]{1,0:T(4,128)S(1)}, f32[4,2048]{1,0:T(4,128)S(1)}, u32[]{:S(2)}, u32[]{:S(2)}) collective-permute-start(f32[4,2048]{1,0:T(4,128)S(1)} %get-tuple-element.468), channel_id=1, source_target_pairs={{0,4},{1,5},{2,6},{3,7},{4,0},{5,1},{6,2},{7,3},{8,12},{9,13},{10,... | collective-permute-start | bytes 98312 | tf_op jit(solution)/shard_map/ppermute | solution.py:279
  220.5 7.2 %collective-permute-start.14 = (f32[4,2048]{1,0:T(4,128)S(1)}, f32[4,2048]{1,0:T(4,128)S(1)}, u32[]{:S(2)}, u32[]{:S(2)}) collective-permute-start(f32[4,2048]{1,0:T(4,128)S(1)} %get-tuple-element.469), channel_id=1, source_target_pairs={{0,2},{1,3},{2,0},{3,1},{4,6},{5,7},{6,4},{7,5},{8,10},{9,11},{10,... | collective-permute-start | bytes 98312 | tf_op jit(solution)/shard_map/ppermute | solution.py:279
